TPU v7x, 256 devices: a whole 4x4x8 slice. The times are simulated.
256 devices in a mesh: tiles: 64 (over x, z, core), sub: 4 (over y).
Axes of the slice: x: 4, y: 4, z: 8, core: 2. Of those that a mesh axis runs over, the one named last changes fastest.
Arguments:
- floe_area: float32 [5, 16, 32, 32768], P(None, None, 'sub', 'tiles'), may hold values from 0 to 1
- courant: float32 [2, 32, 32768], P(None, 'sub', 'tiles'), may hold values from -0.45 to 0.45
- spectra: bfloat16 [64, 4, 512, 1296], P('tiles', 'sub'), may hold values from 0.0049743652 to 0.5
- send_rows: int32 [64, 4, 64, 4, 4], P('tiles', 'sub'), may hold values from 0 to 511
- src_slot: int32 [4, 32, 32768], P(None, 'sub', 'tiles'), may hold values from 0 to 1023
- src_weight: float32 [4, 32, 32768], P(None, 'sub', 'tiles'), may hold values from 0.1 to 0.5
- thickness: float32 [32, 32768], P('sub', 'tiles'), may hold values from 0.3 to 3
- edge_angle: float32 [32, 32768], P('sub', 'tiles'), may hold values from -3.140625 to 3.140625
- decay_rate: float32 [36], replicated, may hold values from 0.05 to 0.5
- strain_table: bfloat16 [16, 1296], replicated, may hold values from 0.0009994507 to 1
- ice_mask: int32 [32, 32768], P('sub', 'tiles'), may hold values 0 or 1
- break_bin: int32 [32, 32768], P('sub', 'tiles'), may hold values from 1 to 15
Outputs:
- fractured: float32 [5, 16, 32, 32768], P(None, None, 'sub', 'tiles')
Inputs may be any that keep to these rules, and one draw needn't show every extreme that they name: `send_rows`: wave cells numbered within the sending device; every device sends exactly 4 spectra to every device. `src_slot`: slots numbered in the order of the sending device's tiles index, then its sub index, then the slot.
All inputs are finite; a program needn't handle non-finite values. No bound on the sum of `ice_mask` on one device may be relied on, other than what follows from the above.
Results may differ from a plain program's by a relative error of at most 0.0003.
Values may be sent and summed in bfloat16 or wider, within the bound.
A program may use at most 64 MiB of HBM per device.

v0:
```python
import math

import jax
import jax.numpy as jnp
from jax import lax
from jax.sharding import PartitionSpec as P

NDIR = 36
NSUB = 3


def with_halo(shard, sides, width):
    for axis, dim in sides:
        size, length = (lax.axis_size(axis), shard.shape[dim])
        up = [(i, (i + 1) % size) for i in range(size)]
        down = [(j, i) for i, j in up]
        last = lax.slice_in_dim(shard, length - width, length, axis=dim)
        initial = lax.slice_in_dim(shard, 0, width, axis=dim)
        before = lax.ppermute(last, axis, up)
        after = lax.ppermute(initial, axis, down)
        shard = jnp.concatenate([before, shard, after], axis=dim)
    return shard


def damping_flat(decay_rate, thick_cells, edge_cells, dir_count, bin_count):
    bin_index = jnp.arange(bin_count, dtype=jnp.int32)
    direction = (bin_index % dir_count).astype(jnp.float32)
    angles = 2.0 * math.pi * direction / dir_count - math.pi
    decay_bins = jnp.repeat(decay_rate, dir_count)
    cosine = jnp.cos(angles[None, :] - edge_cells[:, None])
    path_length = 1.0 / (0.25 + 0.75 * cosine * cosine)
    exponent = decay_bins[None, :] * thick_cells[:, None] * path_length
    return jnp.exp(-exponent)


def fracture(moved, hist, ice_cells, break_cells, bin_count):
    total_hist = jnp.sum(hist, axis=0)
    hist_share = hist / total_hist
    strength = (
        ice_cells.astype(jnp.float32)
        * total_hist
        / (total_hist + 0.005 * hist.shape[0] * bin_count)
    )
    shorter = jnp.cumsum(hist_share, axis=0) - hist_share
    size_bins = jnp.arange(hist.shape[0], dtype=jnp.int32)[:, None]
    allowed = (size_bins >= break_cells[None, :]).astype(jnp.float32)
    breakable = moved * allowed[None]
    above_sum = jnp.sum(breakable, axis=1, keepdims=True) - jnp.cumsum(breakable, axis=1)
    return (
        moved - breakable * (strength * shorter)[None] + above_sum * (strength * hist_share)[None]
    )


def advance(extended, courant_ext):
    east_part = jnp.maximum(courant_ext[0], 0.0)
    west_part = jnp.maximum(-courant_ext[0], 0.0)
    north_part = jnp.maximum(courant_ext[1], 0.0)
    south_part = jnp.maximum(-courant_ext[1], 0.0)
    keep_part = (1.0 - east_part - west_part - north_part - south_part)[1:-1, 1:-1]
    result = extended[:, 1:-1, 1:-1] * keep_part
    result = result + (extended * east_part)[:, 1:-1, :-2]
    result = result + (extended * west_part)[:, 1:-1, 2:]
    result = result + (extended * north_part)[:, :-2, 1:-1]
    result = result + (extended * south_part)[:, 2:, 1:-1]
    return result


def row_valid(width, row_count):
    position = (
        lax.axis_index("sub") * row_count
        + jnp.arange(row_count + 2 * width, dtype=jnp.int32)
        - width
    )
    inside = (position >= 0) & (position < lax.axis_size("sub") * row_count)
    return inside.astype(jnp.float32)[None, :, None]


def shards(
    floe_area,
    courant,
    spectra,
    send_rows,
    src_slot,
    src_weight,
    thickness,
    edge_angle,
    decay_rate,
    strain_table,
    ice_mask,
    break_bin,
):
    cat_count, fsd_count, row_count, col_count = floe_area.shape
    layer_count = cat_count * fsd_count
    joined = jnp.concatenate(
        [floe_area.reshape(layer_count, row_count, col_count), courant], axis=0
    )
    widened = with_halo(joined, (("tiles", 2), ("sub", 1)), 1) * row_valid(1, row_count)
    courant_ext = widened[layer_count:]
    moved = advance(widened[:layer_count], courant_ext)
    for substep in range(1, NSUB):
        widened_area = with_halo(moved, (("tiles", 2), ("sub", 1)), 1) * row_valid(1, row_count)
        moved = advance(widened_area, courant_ext)
    own_waves = spectra[0, 0]
    bin_count = own_waves.shape[1]
    outgoing = own_waves[send_rows[0, 0]]
    incoming = lax.all_to_all(
        lax.all_to_all(outgoing, "tiles", split_axis=0, concat_axis=0, tiled=True),
        "sub",
        split_axis=1,
        concat_axis=1,
        tiled=True,
    )
    received = incoming.reshape(-1, bin_count)
    cell_count = row_count * col_count
    block_size = math.gcd(cell_count, 512)
    block_count = cell_count // block_size
    source_count = src_slot.shape[0]
    slot_cells = src_slot.reshape(source_count, cell_count)
    weight_cells = src_weight.reshape(source_count, cell_count)
    thick_cells = thickness.reshape(cell_count)
    edge_cells = edge_angle.reshape(cell_count)

    def one_block(block_number, hist_all):
        start = block_number * block_size
        slot_block = lax.dynamic_slice_in_dim(slot_cells, start, block_size, 1)
        weight_block = lax.dynamic_slice_in_dim(weight_cells, start, block_size, 1)
        thick_block = lax.dynamic_slice_in_dim(thick_cells, start, block_size, 0)
        edge_block = lax.dynamic_slice_in_dim(edge_cells, start, block_size, 0)
        spectrum = weight_block[0][:, None] * received[slot_block[0]].astype(jnp.float32)
        for source in range(1, source_count):
            spectrum = spectrum + weight_block[source][:, None] * received[
                slot_block[source]
            ].astype(jnp.float32)
        attenuated = (
            spectrum * damping_flat(decay_rate, thick_block, edge_block, NDIR, bin_count)
        ).astype(jnp.bfloat16)
        block_hist = lax.dot_general(
            strain_table, attenuated, (((1,), (1,)), ((), ())), preferred_element_type=jnp.float32
        )
        return lax.dynamic_update_slice_in_dim(hist_all, block_hist, start, 1)

    hist = lax.fori_loop(0, block_count, one_block, jnp.zeros((fsd_count, cell_count), jnp.float32))
    fractured = fracture(
        moved.reshape(cat_count, fsd_count, cell_count),
        hist,
        ice_mask.reshape(-1),
        break_bin.reshape(-1),
        bin_count,
    )
    return fractured.reshape(cat_count, fsd_count, row_count, col_count)


def solution(mesh):
    in_specs = (
        P(None, None, "sub", "tiles"),
        P(None, "sub", "tiles"),
        P("tiles", "sub", None, None),
        P("tiles", "sub", None, None, None),
        P(None, "sub", "tiles"),
        P(None, "sub", "tiles"),
        P("sub", "tiles"),
        P("sub", "tiles"),
        P(),
        P(),
        P("sub", "tiles"),
        P("sub", "tiles"),
    )
    out_specs = P(None, None, "sub", "tiles")
    return jax.shard_map(shards, mesh=mesh, in_specs=in_specs, out_specs=out_specs, check_vma=False)
```

profile of v0, /device:TPU:1, one launch (start us, length us, event | category | flops | bytes accessed | tf_op | source)
XLA Modules:
  0.0 408.2 jit_solution(1852248745108352592)
XLA Ops:
  2.1 5.6 %gather_fusion.4 = bf16[1024,1296]{1,0:T(8,128)(2,1)} fusion(bf16[512,1296]{1,0:T(8,128)(2,1)S(1)} %bitcast.89, s32[1024]{0:T(1024)S(1)} %broadcast_clamp_fusion), kind=kCustom, calls=%fused_computation.4 | custom fusion | bytes 5312512 | tf_op jit(solution)/shard_map/gather | solution.py:105
  7.7 5.8 %reshape.352 = bf16[64,4,4,1296]{3,2,1,0:T(4,128)(2,1)} reshape(bf16[1024,1296]{1,0:T(8,128)(2,1)} %gather_fusion.4) | data formatting | bytes 5308416 | tf_op jit(solution)/shard_map/gather | solution.py:105
  13.5 13.3 %all-to-all-start = ((bf16[64,4,4,1296]{3,2,1,0:T(4,128)(2,1)}), bf16[64,4,4,1296]{3,2,1,0:T(4,128)(2,1)}, u32[]{:S(2)}, u32[]{:S(2)}) async-start(bf16[64,4,4,1296]{3,2,1,0:T(4,128)(2,1)} %reshape.352), calls=%async_computation | async-start | bytes 5767168 | tf_op jit(solution)/shard_map/all_to_all | solution.py:107
  28.8 65.7 %collective-permute-done.1 = f32[82,8,1]{2,1,0:T(8,128)S(1)} collective-permute-done((f32[82,8,1]{2,1,0:T(8,128)S(1)}, f32[82,8,1]{2,1,0:T(8,128)S(1)}, u32[]{:S(2)}, u32[]{:S(2)}) %collective-permute-start.1) | collective-permute-done | bytes 2656 | tf_op jit(solution)/shard_map/ppermute | solution.py:20
  101.2 3.1 collective-permute-done.2
  107.8 5.5 %collective-permute-start.5 = (f32[80,8,1]{2,1,0:T(8,128)S(1)}, f32[80,8,1]{2,1,0:T(8,128)S(1)}, u32[]{:S(2)}, u32[]{:S(2)}) collective-permute-start(f32[80,8,1]{2,1,0:T(8,128)S(1)} %get-tuple-element.273), channel_id=1, source_target_pairs={{4,0},{8,4},{12,8},{16,12},{20,16},{24,20},{28,24},{32,28},{36,32}... | collective-permute-start | bytes 7688 | tf_op jit(solution)/shard_map/ppermute | solution.py:20
  113.3 3.1 collective-permute-done.5
  120.0 4.4 %copy.18 = bf16[64,4,4,1296]{3,2,0,1:T(4,128)(2,1)} copy(bf16[64,4,4,1296]{3,2,1,0:T(4,128)(2,1)} %all-to-all-done) | data formatting | bytes 5308416 | tf_op jit(solution)/shard_map/all_to_all | solution.py:107
  124.4 4.6 %all-to-all-start.1 = ((bf16[64,4,4,1296]{3,2,0,1:T(4,128)(2,1)}), bf16[64,4,4,1296]{3,2,0,1:T(4,128)(2,1)}, u32[]{:S(2)}, u32[]{:S(2)}) async-start(bf16[64,4,4,1296]{3,2,0,1:T(4,128)(2,1)} %copy.18), calls=%async_computation.1 | async-start | bytes 5767168 | tf_op jit(solution)/shard_map/all_to_all | solution.py:106
  132.1 6.7 %collective-permute-start.9 = (f32[80,8,1]{2,1,0:T(8,128)S(1)}, f32[80,8,1]{2,1,0:T(8,128)S(1)}, u32[]{:S(2)}, u32[]{:S(2)}) collective-permute-start(f32[80,8,1]{2,1,0:T(8,128)S(1)} %get-tuple-element.271), channel_id=1, source_target_pairs={{4,0},{8,4},{12,8},{16,12},{20,16},{24,20},{28,24},{32,28},{36,32}... | collective-permute-start | bytes 7688 | tf_op jit(solution)/shard_map/ppermute | solution.py:20
  143.9 3.0 collective-permute-start.11
  146.9 13.3 %collective-permute-done.11 = f32[80,1,514]{2,1,0:T(1,128)S(1)} collective-permute-done((f32[80,1,514]{2,1,0:T(1,128)S(1)}, f32[80,1,514]{2,1,0:T(1,128)S(1)}, u32[]{:S(2)}, u32[]{:S(2)}) %collective-permute-start.11) | collective-permute-done | bytes 164512 | tf_op jit(solution)/shard_map/ppermute | solution.py:20
  164.8 4.4 %copy.19 = bf16[64,4,4,1296]{3,2,1,0:T(4,128)(2,1)} copy(bf16[64,4,4,1296]{3,2,0,1:T(4,128)(2,1)} %all-to-all-done.1) | data formatting | bytes 5308416 | tf_op jit(solution)/shard_map/all_to_all | solution.py:106
  169.2 4.3 %reshape.315 = bf16[1024,1296]{1,0:T(8,128)(2,1)S(1)} reshape(bf16[64,4,4,1296]{3,2,1,0:T(4,128)(2,1)} %copy.19) | data formatting | bytes 5308416 | tf_op jit(solution)/shard_map/reshape | solution.py:113
  173.5 231.9 %while.15 = (s32[]{:T(128)}, f32[16,4096]{1,0:T(8,128)S(1)}, f32[4,4096]{1,0:T(4,128)}, s32[4,4096]{1,0:T(4,128)}, bf16[1024,1296]{1,0:T(8,128)(2,1)S(1)}, /*ind...) while((s32[]{:T(128)}, f32[16,4096]{1,0:T(8,128)S(1)}, ...), condition=%wide.region_1.2_spmd, body=%wide.region_0.1_spmd.sunk | while | flops 35190168 | bytes 16123051 | solution.py:142
  174.5 2.9 gather_fusion
  180.4 2.9 gather_fusion.2
  183.3 3.0 gather_fusion.3
  188.9 13.6 %fusion.56 = f32[16,4096]{1,0:T(8,128)S(1)} fusion(f32[16,4096]{1,0:T(8,128)S(1)} %get-tuple-element.364, s32[]{:T(128)S(6)} %select_n.134, bf16[16,1296]{1,0:T(8,128)(2,1)} %get-tuple-element.387, bf16[512,1296]{1,0:T(8,128)(2,1)} %gather_fusion, bf16[512,1296]{1,0:T(8,128)(2,1)} %gather_fusion.1, bf16[512,1296]{1,0:T(8,128)(2,1)} %gather_fusion.2, ...), kind=kOutput, calls=%fused_computation.15.clone.1 | convolution fusion | flops 35168256 | bytes 5411332 | tf_op jit(solution)/shard_map/while/body/eval_jaxpr/dot_general | solution.py:137
  203.5 2.9 gather_fusion
  206.4 2.9 gather_fusion.1
  209.4 2.9 gather_fusion.2
  212.3 3.0 gather_fusion.3
  217.9 13.6 %fusion.56 = f32[16,4096]{1,0:T(8,128)S(1)} fusion(f32[16,4096]{1,0:T(8,128)S(1)} %get-tuple-element.364, s32[]{:T(128)S(6)} %select_n.134, bf16[16,1296]{1,0:T(8,128)(2,1)} %get-tuple-element.387, bf16[512,1296]{1,0:T(8,128)(2,1)} %gather_fusion, bf16[512,1296]{1,0:T(8,128)(2,1)} %gather_fusion.1, bf16[512,1296]{1,0:T(8,128)(2,1)} %gather_fusion.2, ...), kind=kOutput, calls=%fused_computation.15.clone.1 | convolution fusion | flops 35168256 | bytes 5411332 | tf_op jit(solution)/shard_map/while/body/eval_jaxpr/dot_general | solution.py:137
  232.5 2.9 gather_fusion
  238.3 2.9 gather_fusion.2
  241.3 3.0 gather_fusion.3
  246.8 13.6 %fusion.56 = f32[16,4096]{1,0:T(8,128)S(1)} fusion(f32[16,4096]{1,0:T(8,128)S(1)} %get-tuple-element.364, s32[]{:T(128)S(6)} %select_n.134, bf16[16,1296]{1,0:T(8,128)(2,1)} %get-tuple-element.387, bf16[512,1296]{1,0:T(8,128)(2,1)} %gather_fusion, bf16[512,1296]{1,0:T(8,128)(2,1)} %gather_fusion.1, bf16[512,1296]{1,0:T(8,128)(2,1)} %gather_fusion.2, ...), kind=kOutput, calls=%fused_computation.15.clone.1 | convolution fusion | flops 35168256 | bytes 5411332 | tf_op jit(solution)/shard_map/while/body/eval_jaxpr/dot_general | solution.py:137
  261.4 2.9 gather_fusion
  267.3 2.9 gather_fusion.2
  270.2 3.0 gather_fusion.3
  275.8 13.6 %fusion.56 = f32[16,4096]{1,0:T(8,128)S(1)} fusion(f32[16,4096]{1,0:T(8,128)S(1)} %get-tuple-element.364, s32[]{:T(128)S(6)} %select_n.134, bf16[16,1296]{1,0:T(8,128)(2,1)} %get-tuple-element.387, bf16[512,1296]{1,0:T(8,128)(2,1)} %gather_fusion, bf16[512,1296]{1,0:T(8,128)(2,1)} %gather_fusion.1, bf16[512,1296]{1,0:T(8,128)(2,1)} %gather_fusion.2, ...), kind=kOutput, calls=%fused_computation.15.clone.1 | convolution fusion | flops 35168256 | bytes 5411332 | tf_op jit(solution)/shard_map/while/body/eval_jaxpr/dot_general | solution.py:137
  290.4 2.9 gather_fusion
  296.3 2.9 gather_fusion.2
  299.2 3.0 gather_fusion.3
  304.8 13.6 %fusion.56 = f32[16,4096]{1,0:T(8,128)S(1)} fusion(f32[16,4096]{1,0:T(8,128)S(1)} %get-tuple-element.364, s32[]{:T(128)S(6)} %select_n.134, bf16[16,1296]{1,0:T(8,128)(2,1)} %get-tuple-element.387, bf16[512,1296]{1,0:T(8,128)(2,1)} %gather_fusion, bf16[512,1296]{1,0:T(8,128)(2,1)} %gather_fusion.1, bf16[512,1296]{1,0:T(8,128)(2,1)} %gather_fusion.2, ...), kind=kOutput, calls=%fused_computation.15.clone.1 | convolution fusion | flops 35168256 | bytes 5411332 | tf_op jit(solution)/shard_map/while/body/eval_jaxpr/dot_general | solution.py:137
  319.4 2.9 gather_fusion
  325.3 2.9 gather_fusion.2
  328.2 3.0 gather_fusion.3
  333.8 13.6 %fusion.56 = f32[16,4096]{1,0:T(8,128)S(1)} fusion(f32[16,4096]{1,0:T(8,128)S(1)} %get-tuple-element.364, s32[]{:T(128)S(6)} %select_n.134, bf16[16,1296]{1,0:T(8,128)(2,1)} %get-tuple-element.387, bf16[512,1296]{1,0:T(8,128)(2,1)} %gather_fusion, bf16[512,1296]{1,0:T(8,128)(2,1)} %gather_fusion.1, bf16[512,1296]{1,0:T(8,128)(2,1)} %gather_fusion.2, ...), kind=kOutput, calls=%fused_computation.15.clone.1 | convolution fusion | flops 35168256 | bytes 5411332 | tf_op jit(solution)/shard_map/while/body/eval_jaxpr/dot_general | solution.py:137
  348.4 2.9 gather_fusion
  354.3 2.9 gather_fusion.2
  357.2 3.0 gather_fusion.3
  362.8 13.6 %fusion.56 = f32[16,4096]{1,0:T(8,128)S(1)} fusion(f32[16,4096]{1,0:T(8,128)S(1)} %get-tuple-element.364, s32[]{:T(128)S(6)} %select_n.134, bf16[16,1296]{1,0:T(8,128)(2,1)} %get-tuple-element.387, bf16[512,1296]{1,0:T(8,128)(2,1)} %gather_fusion, bf16[512,1296]{1,0:T(8,128)(2,1)} %gather_fusion.1, bf16[512,1296]{1,0:T(8,128)(2,1)} %gather_fusion.2, ...), kind=kOutput, calls=%fused_computation.15.clone.1 | convolution fusion | flops 35168256 | bytes 5411332 | tf_op jit(solution)/shard_map/while/body/eval_jaxpr/dot_general | solution.py:137
  377.4 2.9 gather_fusion
  383.2 2.9 gather_fusion.2
  386.2 3.0 gather_fusion.3
  391.8 13.6 %fusion.56 = f32[16,4096]{1,0:T(8,128)S(1)} fusion(f32[16,4096]{1,0:T(8,128)S(1)} %get-tuple-element.364, s32[]{:T(128)S(6)} %select_n.134, bf16[16,1296]{1,0:T(8,128)(2,1)} %get-tuple-element.387, bf16[512,1296]{1,0:T(8,128)(2,1)} %gather_fusion, bf16[512,1296]{1,0:T(8,128)(2,1)} %gather_fusion.1, bf16[512,1296]{1,0:T(8,128)(2,1)} %gather_fusion.2, ...), kind=kOutput, calls=%fused_computation.15.clone.1 | convolution fusion | flops 35168256 | bytes 5411332 | tf_op jit(solution)/shard_map/while/body/eval_jaxpr/dot_general | solution.py:137
  (183 shorter events, 82.4 us)
Async XLA Ops:
  0.0 1.8 copy-start.11
  13.5 13.3 %copy-start.2 = (f32[5,16,8,512]{3,2,1,0:T(8,128)S(1)}, f32[5,16,8,512]{3,2,1,0:T(8,128)}, u32[]{:S(2)}) copy-start(f32[5,16,8,512]{3,2,1,0:T(8,128)} %param.14) | copy-start | bytes 3932164
  13.5 13.3 %copy-start.3 = (f32[2,8,512]{2,1,0:T(8,128)S(1)}, f32[2,8,512]{2,1,0:T(8,128)}, u32[]{:S(2)}) copy-start(f32[2,8,512]{2,1,0:T(8,128)} %param.15) | copy-start | bytes 98308
  13.5 106.5 %all-to-all-start = ((bf16[64,4,4,1296]{3,2,1,0:T(4,128)(2,1)}), bf16[64,4,4,1296]{3,2,1,0:T(4,128)(2,1)}, u32[]{:S(2)}, u32[]{:S(2)}) async-start(bf16[64,4,4,1296]{3,2,1,0:T(4,128)(2,1)} %reshape.352), calls=%async_computation | async-start | bytes 5767168 | tf_op jit(solution)/shard_map/all_to_all | solution.py:107
  27.0 67.5 %collective-permute-start.1 = (f32[82,8,1]{2,1,0:T(8,128)S(1)}, f32[82,8,1]{2,1,0:T(8,128)S(1)}, u32[]{:S(2)}, u32[]{:S(2)}) collective-permute-start(f32[82,8,1]{2,1,0:T(8,128)S(1)} %get-tuple-element.269), channel_id=1, source_target_pairs={{4,0},{8,4},{12,8},{16,12},{20,16},{24,20},{28,24},{32,28},{36,32}... | collective-permute-start | bytes 7880 | tf_op jit(solution)/shard_map/ppermute | solution.py:20
  27.6 66.9 %collective-permute-start = (f32[82,8,1]{2,1,0:T(8,128)S(1)}, f32[82,8,1]{2,1,0:T(8,128)S(1)}, u32[]{:S(2)}, u32[]{:S(2)}) collective-permute-start(f32[82,8,1]{2,1,0:T(8,128)S(1)} %get-tuple-element.268), channel_id=1, source_target_pairs={{0,4},{4,8},{8,12},{12,16},{16,20},{20,24},{24,28},{28,32},{32,36}... | collective-permute-start | bytes 7880 | tf_op jit(solution)/shard_map/ppermute | solution.py:19
  95.6 5.6 %collective-permute-start.3 = (f32[82,1,514]{2,1,0:T(1,128)S(1)}, f32[82,1,514]{2,1,0:T(1,128)S(1)}, u32[]{:S(2)}, u32[]{:S(2)}) collective-permute-start(f32[82,1,514]{2,1,0:T(1,128)S(1)} %get-tuple-element.263), channel_id=1, source_target_pairs={{1,0},{2,1},{3,2},{0,3},{5,4},{6,5},{7,6},{4,7},{9,8},{10,9},{11,1... | collective-permute-start | bytes 505784 | tf_op jit(solution)/shard_map/ppermute | solution.py:20
  98.4 5.9 %collective-permute-start.2 = (f32[82,1,514]{2,1,0:T(1,128)S(1)}, f32[82,1,514]{2,1,0:T(1,128)S(1)}, u32[]{:S(2)}, u32[]{:S(2)}) collective-permute-start(f32[82,1,514]{2,1,0:T(1,128)S(1)} %get-tuple-element.262), channel_id=1, source_target_pairs={{0,1},{1,2},{2,3},{3,0},{4,5},{5,6},{6,7},{7,4},{8,9},{9,10},{10,1... | collective-permute-start | bytes 505784 | tf_op jit(solution)/shard_map/ppermute | solution.py:19
  106.1 7.2 %copy-start.4 = (s32[8,512]{1,0:T(8,128)S(1)}, s32[8,512]{1,0:T(8,128)}, u32[]{:S(2)}) copy-start(s32[8,512]{1,0:T(8,128)} %param.25) | copy-start | bytes 49156
  107.8 8.6 %collective-permute-start.5 = (f32[80,8,1]{2,1,0:T(8,128)S(1)}, f32[80,8,1]{2,1,0:T(8,128)S(1)}, u32[]{:S(2)}, u32[]{:S(2)}) collective-permute-start(f32[80,8,1]{2,1,0:T(8,128)S(1)} %get-tuple-element.273), channel_id=1, source_target_pairs={{4,0},{8,4},{12,8},{16,12},{20,16},{24,20},{28,24},{32,28},{36,32}... | collective-permute-start | bytes 7688 | tf_op jit(solution)/shard_map/ppermute | solution.py:20
  113.3 4.0 collective-permute-start.4
  118.4 10.6 %collective-permute-start.7 = (f32[80,1,514]{2,1,0:T(1,128)S(1)}, f32[80,1,514]{2,1,0:T(1,128)S(1)}, u32[]{:S(2)}, u32[]{:S(2)}) collective-permute-start(f32[80,1,514]{2,1,0:T(1,128)S(1)} %get-tuple-element.267), channel_id=1, source_target_pairs={{1,0},{2,1},{3,2},{0,3},{5,4},{6,5},{7,6},{4,7},{9,8},{10,9},{11,1... | collective-permute-start | bytes 493448 | tf_op jit(solution)/shard_map/ppermute | solution.py:20
  118.5 10.5 %collective-permute-start.6 = (f32[80,1,514]{2,1,0:T(1,128)S(1)}, f32[80,1,514]{2,1,0:T(1,128)S(1)}, u32[]{:S(2)}, u32[]{:S(2)}) collective-permute-start(f32[80,1,514]{2,1,0:T(1,128)S(1)} %get-tuple-element.266), channel_id=1, source_target_pairs={{0,1},{1,2},{2,3},{3,0},{4,5},{5,6},{6,7},{7,4},{8,9},{9,10},{10,1... | collective-permute-start | bytes 493448 | tf_op jit(solution)/shard_map/ppermute | solution.py:19
  124.4 40.3 %all-to-all-start.1 = ((bf16[64,4,4,1296]{3,2,0,1:T(4,128)(2,1)}), bf16[64,4,4,1296]{3,2,0,1:T(4,128)(2,1)}, u32[]{:S(2)}, u32[]{:S(2)}) async-start(bf16[64,4,4,1296]{3,2,0,1:T(4,128)(2,1)} %copy.18), calls=%async_computation.1 | async-start | bytes 5767168 | tf_op jit(solution)/shard_map/all_to_all | solution.py:106
  130.4 8.4 %copy-start.7 = (s32[8,512]{1,0:T(8,128)S(1)}, s32[8,512]{1,0:T(8,128)}, u32[]{:S(2)}) copy-start(s32[8,512]{1,0:T(8,128)} %param.24) | copy-start | bytes 49156
  130.4 8.4 %copy-start.5 = (f32[4,8,512]{2,1,0:T(8,128)S(1)}, f32[4,8,512]{2,1,0:T(8,128)}, u32[]{:S(2)}) copy-start(f32[4,8,512]{2,1,0:T(8,128)} %param.19) | copy-start | bytes 196612
  131.9 7.6 %copy-start.6 = (s32[4,8,512]{2,1,0:T(8,128)S(1)}, s32[4,8,512]{2,1,0:T(8,128)}, u32[]{:S(2)}) copy-start(s32[4,8,512]{2,1,0:T(8,128)} %param.18) | copy-start | bytes 196612
  131.9 8.3 %copy-start.8 = (f32[8,512]{1,0:T(8,128)S(1)}, f32[8,512]{1,0:T(8,128)}, u32[]{:S(2)}) copy-start(f32[8,512]{1,0:T(8,128)} %param.20) | copy-start | bytes 49156
  131.9 8.9 %copy-start.9 = (f32[8,512]{1,0:T(8,128)S(1)}, f32[8,512]{1,0:T(8,128)}, u32[]{:S(2)}) copy-start(f32[8,512]{1,0:T(8,128)} %param.21) | copy-start | bytes 49156
  132.1 9.3 %collective-permute-start.9 = (f32[80,8,1]{2,1,0:T(8,128)S(1)}, f32[80,8,1]{2,1,0:T(8,128)S(1)}, u32[]{:S(2)}, u32[]{:S(2)}) collective-permute-start(f32[80,8,1]{2,1,0:T(8,128)S(1)} %get-tuple-element.271), channel_id=1, source_target_pairs={{4,0},{8,4},{12,8},{16,12},{20,16},{24,20},{28,24},{32,28},{36,32}... | collective-permute-start | bytes 7688 | tf_op jit(solution)/shard_map/ppermute | solution.py:20
  138.8 4.0 collective-permute-start.8
  143.9 16.3 %collective-permute-start.11 = (f32[80,1,514]{2,1,0:T(1,128)S(1)}, f32[80,1,514]{2,1,0:T(1,128)S(1)}, u32[]{:S(2)}, u32[]{:S(2)}) collective-permute-start(f32[80,1,514]{2,1,0:T(1,128)S(1)} %get-tuple-element.265), channel_id=1, source_target_pairs={{1,0},{2,1},{3,2},{0,3},{5,4},{6,5},{7,6},{4,7},{9,8},{10,9},{11,1... | collective-permute-start | bytes 493448 | tf_op jit(solution)/shard_map/ppermute | solution.py:20
  146.9 14.0 %collective-permute-start.10 = (f32[80,1,514]{2,1,0:T(1,128)S(1)}, f32[80,1,514]{2,1,0:T(1,128)S(1)}, u32[]{:S(2)}, u32[]{:S(2)}) collective-permute-start(f32[80,1,514]{2,1,0:T(1,128)S(1)} %get-tuple-element.264), channel_id=1, source_target_pairs={{0,1},{1,2},{2,3},{3,0},{4,5},{5,6},{6,7},{7,4},{8,9},{9,10},{10,1... | collective-permute-start | bytes 493448 | tf_op jit(solution)/shard_map/ppermute | solution.py:19
  163.6 1.1 copy-start
  169.2 4.4 %copy-start.10 = (f32[36]{0:T(128)S(1)}, f32[36]{0:T(128)}, u32[]{:S(2)}) copy-start(f32[36]{0:T(128)} %param.22) | copy-start | bytes 436
  405.5 1.3 copy-start.1
where the time goes:
time: 416 us; the launch traced here: 408 us
  local copies, waits for them, and re-layouts  146 us (35%)
  matrix products  109 us (26%)
  waiting for transfers between devices  91 us (22%)
  starting transfers between devices  39.3 us (9%)
  other arithmetic  21.9 us (5%)
    dot_general x8, matrix products, one_block(): lax.dot_general(strain_table, attenuated, (((1,), (1,)), ((), ())), prefe...  109 us
    ppermute x6, waiting for transfers between devices, with_halo(): after = lax.ppermute(initial, axis, down)  84.8 us
    gather x24, local copies, waits for them, and re-layouts, one_block(): received[slot_block[source]].astype(jnp.float32)  70.2 us
    gather x8, local copies, waits for them, and re-layouts, one_block(): received[slot_block[0]].astype(jnp.float32)  23.7 us
    ppermute x6, starting transfers between devices, with_halo(): after = lax.ppermute(initial, axis, down)  18.7 us
    all_to_all x1, starting transfers between devices, shards(): lax.all_to_all(outgoing, 'tiles', split_axis=0, concat_axis=0, tiled=True)  13.3 us
    gather x2, local copies, waits for them, and re-layouts, shards(): outgoing = own_waves[send_rows[0, 0]]  11.3 us
  transfers between devices with their start and end apart: 14, of which 8 were waited for; matrix products, arithmetic and copies ran while one was open for 5% of the time, Pallas kernels for 0%

commit v1 on v0

v1 whole, which is shorter than its diff:
```python
import functools
import math

import jax
import jax.numpy as jnp
from jax import lax
from jax.experimental import pallas as pl
from jax.experimental.pallas import tpu as pltpu
from jax.sharding import PartitionSpec as P

MESH = pl.DeviceIdType.MESH
F32 = jnp.float32
BF16 = jnp.bfloat16
NDIR = 36
NBIN = 1296
NSUB = 3
N_DEV = 256
SPLIT = 1024
TAIL = 384


def coords():
    t, s = lax.axis_index("tiles"), lax.axis_index("sub")
    return t // 16, lax.rem(t, 16), s


def zc_peer(i, x, zc, s):
    c = lax.rem(lax.rem(zc, 2) + i % 2, 2)
    z = lax.rem(zc // 2 + i // 2, 8)
    return (x * 16 + z * 2 + c, s)


def xy_peer(i, x, zc, s):
    return (lax.rem(x + i // 4, 4) * 16 + zc, lax.rem(s + i % 4, 4))


def exchange_kernel(xa, xb, ra, rb, send_sem, recv_a, recv_b, own_sem, group_sem):
    x, zc, s = coords()
    me = (x * 16 + zc) * 4 + s
    barrier = pltpu.get_barrier_semaphore()
    for i in range(1, 16):
        pl.semaphore_signal(barrier, inc=1, device_id=zc_peer(i, x, zc, s), device_id_type=MESH)
        pl.semaphore_signal(barrier, inc=1, device_id=xy_peer(i, x, zc, s), device_id_type=MESH)
    pl.semaphore_wait(barrier, 30)
    for i in range(1, 16):
        pl.semaphore_signal(group_sem, inc=1, device_id=xy_peer(i, x, zc, s), device_id_type=MESH)
    pl.semaphore_wait(group_sem, 15)
    own_a = pltpu.make_async_copy(xa.at[me], ra.at[me], own_sem.at[0])
    own_b = pltpu.make_async_copy(xb.at[me], rb.at[me], own_sem.at[1])
    own_a.start()
    own_b.start()

    def sender(src, dst, sem, slot):
        def one(i, carry):
            c = lax.rem(lax.rem(zc, 2) + lax.rem(i, 2), 2)
            z = lax.rem(zc // 2 + lax.rem(i // 2, 8), 8)
            tile = lax.rem(x + i // 64, 4) * 16 + z * 2 + c
            sub = lax.rem(s + lax.rem(i // 16, 4), 4)
            pltpu.make_async_remote_copy(
                src_ref=src.at[tile * 4 + sub],
                dst_ref=dst.at[me],
                send_sem=send_sem.at[slot],
                recv_sem=sem,
                device_id=(tile, sub),
                device_id_type=MESH,
            ).start()
            return carry

        lax.fori_loop(1, N_DEV, one, 0)

    sender(xa, ra, recv_a, 0)
    sender(xb, rb, recv_b, 1)
    own_a.wait()
    own_b.wait()
    rest = pl.ds(0, N_DEV - 1)
    pltpu.make_async_copy(xa.at[rest], ra.at[rest], recv_a).wait()
    pltpu.make_async_copy(xb.at[rest], rb.at[rest], recv_b).wait()
    pltpu.make_async_copy(xa.at[rest], ra.at[rest], send_sem.at[0]).wait()
    pltpu.make_async_copy(xb.at[rest], rb.at[rest], send_sem.at[1]).wait()


def exchange(xa, xb):
    vmem = pl.BlockSpec(memory_space=pltpu.VMEM)
    return pl.pallas_call(
        exchange_kernel,
        out_shape=[jax.ShapeDtypeStruct(v.shape, v.dtype) for v in (xa, xb)],
        in_specs=[vmem] * 2,
        out_specs=[vmem] * 2,
        scratch_shapes=[
            pltpu.SemaphoreType.DMA((2,)),
            pltpu.SemaphoreType.DMA(()),
            pltpu.SemaphoreType.DMA(()),
            pltpu.SemaphoreType.DMA((2,)),
            pltpu.SemaphoreType.REGULAR,
        ],
        compiler_params=pltpu.CompilerParams(
            collective_id=0, has_side_effects=True, vmem_limit_bytes=50 << 20
        ),
    )(xa, xb)


def transpose_in(src, table, first, width):
    for lane in range(0, width, 128):
        size = min(128, width - lane)
        block = src[:, :, lane : lane + 128].reshape(N_DEV * 4, 128)
        turned = block.T
        table[first + lane : first + lane + size, :] = turned[:size]


def build_mixing(r, slot, weight, mixing):
    rows = lax.broadcasted_iota(jnp.int32, (N_DEV * 4, 512), 0).astype(jnp.int16)
    total = jnp.zeros((N_DEV * 4, 512), BF16)
    for k in range(4):
        slots = slot[k, pl.ds(r, 1), :].astype(jnp.int16)
        weights = weight[k, pl.ds(r, 1), :].astype(BF16)
        total = total + jnp.where(rows == slots, weights, jnp.zeros((), BF16))
    mixing[...] = total


def wide(column, lanes=4):
    return jnp.concatenate([column] * lanes, axis=1)


def fill_decay(decay, decay_table):
    row = lax.broadcasted_iota(jnp.int32, (72, 128), 0)
    for g in range(18):
        decay_table[g * 72 : g * 72 + 72, :] = jnp.where(row < 36, decay[2 * g], decay[2 * g + 1])


def path_table(r, thick, edge, trig):
    edge_row = edge[pl.ds(r, 1), :]
    cos_row, sin_row = jnp.cos(edge_row), jnp.sin(edge_row)
    cosine = wide(trig[0]) * cos_row + wide(trig[1]) * sin_row
    return (-math.log2(math.e) * thick[pl.ds(r, 1), :]) / (0.25 + 0.75 * cosine * cosine)


def attenuate(first, size, table, mixing, decay_table, path, att):
    step = 144
    for start in range(first, first + size, step):
        spectrum = jnp.dot(table[start : start + step, :], mixing[...], preferred_element_type=F32)
        decay_rows = wide(decay_table[start : start + step, :])
        damping = jnp.exp2(decay_rows * jnp.concatenate([path] * (step // 72), axis=0))
        att[start : start + step, :] = (spectrum * damping).astype(BF16)


def fracture(hist, weight, ice, brk, moved, out):
    total_w = weight[0] + weight[1] + weight[2] + weight[3]
    used_w = sum(weight[k].astype(BF16).astype(F32) for k in range(4))
    fix = total_w / used_w
    rows = [hist[j] * fix for j in range(16)]
    total = functools.reduce(jnp.add, rows)
    strength = ice[...].astype(F32) * total / (total + 0.005 * 16 * NBIN)
    scale = strength / total
    share = [v * scale for v in rows]
    shorter, run = [], jnp.zeros_like(total)
    for j in range(16):
        shorter.append(run)
        run = run + share[j]
    brk_rows = brk[...]
    for n in range(5):
        above = jnp.zeros_like(total)
        for k in range(15, -1, -1):
            value = moved[n, k]
            breakable = jnp.where(brk_rows <= k, value, 0.0)
            out[n, k] = value - breakable * shorter[k] + above * share[k]
            above = above + breakable


def remap_kernel(
    decay, ra, rb, slot, weight, thick, edge, strain, ice, brk, moved, trig, out,
    table, mixing, decay_table, att, hist
):
    fill_decay(decay, decay_table)
    transpose_in(ra, table, 0, SPLIT)
    transpose_in(rb, table, SPLIT, NBIN - SPLIT)

    def one_row(r, carry):
        build_mixing(r, slot, weight, mixing)
        path = path_table(r, thick, edge, trig)
        attenuate(0, NBIN, table, mixing, decay_table, path, att)
        row_hist = jnp.dot(strain[...], att[...], preferred_element_type=F32)
        hist[:, pl.ds(r, 1), :] = row_hist[:, None, :]
        return carry

    lax.fori_loop(0, 8, one_row, 0)
    fracture(hist, weight, ice, brk, moved, out)


def remap(ra, rb, slot, weight, thick, edge, decay, strain, ice, brk, moved):
    angles = 2.0 * math.pi * (jnp.arange(72) % NDIR).astype(F32) / NDIR - math.pi
    trig = jnp.broadcast_to(jnp.stack([jnp.cos(angles), jnp.sin(angles)])[:, :, None], (2, 72, 128))
    vmem = pl.BlockSpec(memory_space=pltpu.VMEM)
    return pl.pallas_call(
        remap_kernel,
        out_shape=jax.ShapeDtypeStruct(moved.shape, F32),
        in_specs=[pl.BlockSpec(memory_space=pltpu.SMEM)] + [vmem] * 11,
        out_specs=vmem,
        scratch_shapes=[
            pltpu.VMEM((NBIN, N_DEV * 4), BF16),
            pltpu.VMEM((N_DEV * 4, 512), BF16),
            pltpu.VMEM((NBIN, 128), F32),
            pltpu.VMEM((NBIN, 512), BF16),
            pltpu.VMEM((16, 8, 512), F32),
        ],
        compiler_params=pltpu.CompilerParams(vmem_limit_bytes=50 << 20),
    )(decay, ra, rb, slot, weight, thick, edge, strain, ice, brk, moved, trig)


def transport_kernel(ext, out):
    east = jnp.maximum(ext[80], 0.0)
    west = jnp.maximum(-ext[80], 0.0)
    north = jnp.maximum(ext[81], 0.0)
    south = jnp.maximum(-ext[81], 0.0)
    keep = 1.0 - east - west - north - south

    def one(layer, carry):
        v = ext[layer]
        for _ in range(NSUB):
            v = (
                v * keep
                + pltpu.roll(v * east, 1, 1)
                + pltpu.roll(v * west, 639, 1)
                + pltpu.roll(v * north, 1, 0)
                + pltpu.roll(v * south, 15, 0)
            )
        out[layer] = v[0:8, 0:512]
        return carry

    lax.fori_loop(0, 80, one, 0)


def transport(floe, courant):
    joined = jnp.concatenate([floe.reshape(80, 8, 512), courant], axis=0)
    n_sub, n_tiles = lax.axis_size("sub"), lax.axis_size("tiles")
    below = lax.ppermute(joined[:, 0:3], "sub", [(i + 1, i) for i in range(n_sub - 1)])
    above = lax.ppermute(joined[:, 5:8], "sub", [(i, i + 1) for i in range(n_sub - 1)])
    rows = jnp.concatenate([joined, below, jnp.zeros((82, 2, 512), F32), above], axis=1)
    right = lax.ppermute(rows[:, :, 0:3], "tiles", [((i + 1) % n_tiles, i) for i in range(n_tiles)])
    left = lax.ppermute(rows[:, :, 509:], "tiles", [(i, (i + 1) % n_tiles) for i in range(n_tiles)])
    ext = jnp.concatenate([rows, right, jnp.zeros((82, 16, 122), F32), left], axis=2)
    return pl.pallas_call(
        transport_kernel,
        out_shape=jax.ShapeDtypeStruct((80, 8, 512), F32),
        in_specs=[pl.BlockSpec(memory_space=pltpu.VMEM)],
        out_specs=pl.BlockSpec(memory_space=pltpu.VMEM),
        compiler_params=pltpu.CompilerParams(vmem_limit_bytes=50 << 20),
    )(ext)


def shards(
    floe_area, courant, spectra, send_rows, src_slot, src_weight, thickness, edge_angle,
    decay_rate, strain_table, ice_mask, break_bin
):
    moved = transport(floe_area, courant).reshape(floe_area.shape)
    picks = send_rows.reshape(N_DEV * 4)
    choose = (picks[:, None] == jnp.arange(512, dtype=jnp.int32)[None, :]).astype(BF16)
    outgoing = jnp.dot(choose, spectra[0, 0], preferred_element_type=F32).astype(BF16)
    outgoing = outgoing.reshape(N_DEV, 4, NBIN)
    tail = jnp.pad(outgoing[:, :, SPLIT:], ((0, 0), (0, 0), (0, SPLIT + TAIL - NBIN)))
    ra, rb = exchange(outgoing[:, :, :SPLIT], tail)
    return remap(
        ra, rb, src_slot, src_weight, thickness, edge_angle, decay_rate, strain_table,
        ice_mask, break_bin, moved
    )


def solution(mesh):
    in_specs = (
        P(None, None, "sub", "tiles"),
        P(None, "sub", "tiles"),
        P("tiles", "sub", None, None),
        P("tiles", "sub", None, None, None),
        P(None, "sub", "tiles"),
        P(None, "sub", "tiles"),
        P("sub", "tiles"),
        P("sub", "tiles"),
        P(),
        P(),
        P("sub", "tiles"),
        P("sub", "tiles"),
    )
    out_specs = P(None, None, "sub", "tiles")
    return jax.shard_map(shards, mesh=mesh, in_specs=in_specs, out_specs=out_specs, check_vma=False)
```

time: 416 us -> 177 us (0.43); the launches traced: 408 us -> 177 us
  Pallas kernels: 0 us -> 124 us
  local copies, waits for them, and re-layouts: 146 us -> 25.6 us
  matrix products: 109 us -> 3.25 us
  waiting for transfers between devices: 91 us -> 3.17 us
  starting transfers between devices: 39.3 us -> 12.5 us
  other arithmetic: 21.9 us -> 7.95 us
    pallas_call x0 -> x3, Pallas kernels: none -> 124 us  [the longest x1 82.3 us: exchange(): pl.pallas_call(exchange_kernel, out_shape=[jax.ShapeDtypeStruct(v.shape,...]
    dot_general x8 -> x1, matrix products: 109 us -> 3.25 us  [shards(): jnp.dot(choose, spectra[0, 0], preferred_element_type=F32).astype(BF16)]
    gather x34 -> x0, local copies, waits for them, and re-layouts: 105 us -> none  [the longest x24 70.2 us: one_block(): received[slot_block[source]].astype(jnp.float32)]
    ppermute x12 -> x4, waiting for transfers between devices: 91 us -> 3.17 us  [the longest x1 2.51 us: transport(): lax.ppermute(joined[:, 0:3], 'sub', [(i + 1, i) for i in range(n_sub - 1)])]
    all_to_all x2 -> x0, starting transfers between devices: 17.9 us -> none  [the longest x1 13.3 us: shards(): lax.all_to_all(outgoing, 'tiles', split_axis=0, concat_axis=0, tiled=True)]
    dynamic_slice x16 -> x0, local copies, waits for them, and re-layouts: 12.1 us -> none  [the longest x8 6.04 us: one_block(): thick_block = lax.dynamic_slice_in_dim(thick_cells, start, block_size, 0)]
    ppermute x12 -> x4, starting transfers between devices: 21.4 us -> 12.5 us  [the longest x1 5.47 us: transport(): lax.ppermute(joined[:, 5:8], 'sub', [(i, i + 1) for i in range(n_sub - 1)])]
    all_to_all x2 -> x0, local copies, waits for them, and re-layouts: 8.81 us -> none  [the longest x1 4.41 us: shards(): lax.all_to_all(outgoing, 'tiles', split_axis=0, concat_axis=0, tiled=True)]
  transfers between devices with their start and end apart: 14 -> 4, of which waited for: 8 -> 2; matrix products, arithmetic and copies ran while one was open for 5% -> 13% of each run, Pallas kernels for 0% -> 47%
where the time goes in v1:
time: 177 us
  Pallas kernels  124 us (70%)
  local copies, waits for them, and re-layouts  25.6 us (14%)
  starting transfers between devices  12.5 us (7%)
  other arithmetic  7.95 us (4%)
  matrix products  3.25 us (2%)
  waiting for transfers between devices  3.17 us (2%)
    pallas_call x1, Pallas kernels, exchange(): pl.pallas_call(exchange_kernel, out_shape=[jax.ShapeDtypeStruct(v.shape,...  82.3 us
    pallas_call x1, Pallas kernels, transport(): pl.pallas_call(transport_kernel, out_shape=jax.ShapeDtypeStruct((80, 8, 5...  21.3 us
    pallas_call x1, Pallas kernels, remap(): pl.pallas_call(remap_kernel, out_shape=jax.ShapeDtypeStruct(moved.shape,...  20.5 us
    reshape x1, local copies, waits for them, and re-layouts, shards(): outgoing = outgoing.reshape(N_DEV, 4, NBIN)  5.74 us
    ppermute x1, starting transfers between devices, transport(): lax.ppermute(joined[:, 5:8], 'sub', [(i, i + 1) for i in range(n_sub - 1)])  5.47 us
    convert_element_type x1, local copies, waits for them, and re-layouts, shards(): jnp.dot(choose, spectra[0, 0], preferred_element_type=F32).astype(BF16)  4.52 us
    concatenate x1, other arithmetic, transport(): jnp.concatenate([rows, right, jnp.zeros((82, 16, 122), F32), left], axis=2)  3.82 us
    ppermute x1, starting transfers between devices, transport(): lax.ppermute(rows[:, :, 0:3], 'tiles', [((i + 1) % n_tiles, i) for i in r...  3.81 us
  transfers between devices with their start and end apart: 4, of which 2 were waited for; matrix products, arithmetic and copies ran while one was open for 13% of the time, Pallas kernels for 47%

profile of v1, /device:TPU:1, one launch (start us, length us, event | category | flops | bytes accessed | tf_op | source)
XLA Modules:
  0.0 176.9 jit_solution(10027328777060485139)
XLA Ops:
  0.0 2.2 %fusion.2 = (f32[82,3,512]{2,1,0:T(4,128)S(1)}, f32[82,3,512]{2,1,0:T(4,128)S(1)}) fusion(f32[80,8,512]{2,1,0:T(8,128)} %bitcast.6, f32[2,8,512]{2,1,0:T(8,128)} %param.13), kind=kLoop, calls=%fused_computation.7 | loop fusion | flops 251904 | bytes 2351104 | tf_op jit(solution)/shard_map/concatenate | solution.py:233
  2.2 0.2 copy.18
  2.3 1.3 collective-permute-start
  3.6 1.0 copy.19
  4.6 5.5 %collective-permute-start.1 = (f32[82,3,512]{2,0,1:T(8,128)}, f32[82,3,512]{2,0,1:T(8,128)}, u32[]{:S(2)}, u32[]{:S(2)}) collective-permute-start(f32[82,3,512]{2,0,1:T(8,128)} %copy.19), channel_id=1, source_target_pairs={{0,1},{1,2},{2,3},{4,5},{5,6},{6,7},{8,9},{9,10},{10,11},{12,13},{... | collective-permute-start | bytes 1511432 | tf_op jit(solution)/shard_map/ppermute | solution.py:236
  10.1 0.1 copy.16
  10.2 0.2 eq.17
  10.4 0.1 fusion.6
  10.4 0.0 copy-done
  10.4 0.0 copy-start.14
  10.4 3.3 %convolution_convert_fusion = bf16[1024,1296]{0,1:T(8,128)(2,1)} fusion(bf16[1,1,512,1296]{2,3,1,0:T(8,128)(2,1)S(1)} %copy-done, s32[1024]{0:T(1024)S(1)} %eq.17), kind=kOutput, calls=%fused_computation | convolution fusion | flops 1360805888 | bytes 3985408 | tf_op jit(solution)/shard_map/dot_general | solution.py:257
  13.7 2.5 %collective-permute-done = f32[82,3,512]{2,0,1:T(8,128)} collective-permute-done((f32[82,3,512]{2,0,1:T(8,128)S(1)}, f32[82,3,512]{2,0,1:T(8,128)}, u32[]{:S(2)}, u32[]{:S(2)}) %collective-permute-start) | collective-permute-done | bytes 503840 | tf_op jit(solution)/shard_map/ppermute | solution.py:235
  16.2 1.4 copy.20
  17.6 0.7 collective-permute-done.1
  18.3 1.4 copy.21
  19.7 0.0 copy-start.12
  19.7 0.1 broadcast_in_dim.6
  19.8 0.7 copy-done.12
  20.5 0.0 copy-done.10
  20.5 1.3 pad_maximum_fusion.5
  21.9 1.4 copy.22
  23.3 3.8 %collective-permute-start.2 = (f32[82,16,3]{0,1,2:T(8,128)S(1)}, f32[82,16,3]{0,1,2:T(8,128)S(1)}, u32[]{:S(2)}, u32[]{:S(2)}) collective-permute-start(f32[82,16,3]{0,1,2:T(8,128)S(1)} %copy.22), channel_id=1, source_target_pairs={{4,0},{8,4},{12,8},{16,12},{20,16},{24,20},{28,24},{32,28},{36,32}... | collective-permute-start | bytes 47240 | tf_op jit(solution)/shard_map/ppermute | solution.py:238
  27.1 0.3 copy.23
  27.4 1.9 %collective-permute-start.3 = (f32[82,16,3]{0,1,2:T(8,128)S(1)}, f32[82,16,3]{0,1,2:T(8,128)S(1)}, u32[]{:S(2)}, u32[]{:S(2)}) collective-permute-start(f32[82,16,3]{0,1,2:T(8,128)S(1)} %copy.23), channel_id=1, source_target_pairs={{0,4},{4,8},{8,12},{12,16},{16,20},{20,24},{24,28},{28,32},{32,36}... | collective-permute-start | bytes 47240 | tf_op jit(solution)/shard_map/ppermute | solution.py:239
  29.3 0.6 pad_maximum_fusion.7
  29.9 4.5 %copy.17 = bf16[1024,1296]{1,0:T(8,128)(2,1)} copy(bf16[1024,1296]{0,1:T(8,128)(2,1)} %convolution_convert_fusion) | data formatting | bytes 5308416 | tf_op jit(solution)/shard_map/convert_element_type | solution.py:257
  34.4 5.7 %reshape.49 = bf16[256,4,1296]{2,1,0:T(4,128)(2,1)} reshape(bf16[1024,1296]{1,0:T(8,128)(2,1)} %copy.17) | data formatting | bytes 5308416 | tf_op jit(solution)/shard_map/reshape | solution.py:258
  40.2 3.7 %slice.24.xa = bf16[256,4,1024]{2,1,0:T(4,128)(2,1)} slice(bf16[256,4,1296]{2,1,0:T(4,128)(2,1)} %reshape.49), slice={[0:256], [0:4], [0:1024]} | slice | bytes 4194304 | tf_op jit(solution)/shard_map/slice | solution.py:260
  43.9 0.7 pad.13.clone
  44.6 0.3 pad.4.xb
  44.9 82.3 %shard_map.118 = (bf16[256,4,1024]{2,1,0:T(4,128)(2,1)S(1)}, bf16[256,4,384]{2,1,0:T(4,128)(2,1)S(1)}) custom-call(bf16[256,4,1024]{2,1,0:T(4,128)(2,1)} %slice.24.xa, bf16[256,4,384]{2,1,0:T(4,128)(2,1)S(1)} %pad.4.xb), custom_call_target="tpu_custom_call" | custom-call | tf_op jit(solution)/shard_map/pallas_call | solution.py:84
  127.3 1.3 copy-done.1
  128.6 0.0 collective-permute-done.2
  128.6 1.2 copy.24
  129.8 0.0 collective-permute-done.3
  129.8 1.2 copy.25
  131.0 3.8 %pad_maximum_fusion.ext = f32[82,16,640]{2,1,0:T(8,128)} fusion(f32[82,16,3]{2,1,0:T(8,128)} %copy.25, f32[82,16,3]{2,1,0:T(8,128)} %copy.24, f32[82,3,512]{2,1,0:T(4,128)} %copy-done.12, f32[82,2,512]{2,1,0:T(2,128)} %copy-done.13, f32[82,3,512]{2,1,0:T(4,128)} %copy-done.11, f32[2,8,512]{2,1,0:T(8,128)S(1)} %copy-done.14, f32[80,8,512]{2,1,0:T(8,128)S(1)} %bitcast.8, ...), kind=kLoop, calls=%fused_computation.1 | loop fusion | flops 5877760 | bytes 6079744 | tf_op jit(solution)/shard_map/concatenate | solution.py:240
  134.8 0.0 copy-start.3
  134.8 0.0 copy-start.4
  134.8 0.0 copy-start.5
  134.9 0.0 copy-start.6
  134.9 0.0 copy-start.7
  134.9 0.0 copy-start.8
  134.9 0.0 copy-start.9
  134.9 21.3 %shard_map.119 = f32[80,8,512]{2,1,0:T(8,128)S(1)} custom-call(f32[82,16,640]{2,1,0:T(8,128)} %pad_maximum_fusion.ext), custom_call_target="tpu_custom_call" | custom-call | tf_op jit(solution)/shard_map/pallas_call | solution.py:241
  156.2 0.1 broadcast_in_dim.15.trig
  156.3 0.0 copy-done.2
  156.4 20.5 %shard_map.120 = f32[5,16,8,512]{3,2,1,0:T(8,128)} custom-call(f32[36]{0:T(128)S(1)} %copy-done.9, bf16[256,4,1024]{2,1,0:T(4,128)(2,1)} %copy-done.1, bf16[256,4,384]{2,1,0:T(4,128)(2,1)S(1)} %get-tuple-element.8.rb, s32[4,8,512]{2,1,0:T(8,128)S(1)} %copy-done.2, f32[4,8,512]{2,1,0:T(8,128)S(1)} %copy-done.3, f32[8,512]{1,0:T(8,128)S(1)} %copy-done.5, ...), custom_call_target="tpu_custom_call" | custom-call | tf_op jit(solution)/shard_map/pallas_call | solution.py:193
  (23 shorter events, 0.0 us)
Async XLA Ops:
  0.0 10.4 %copy-start = (bf16[1,1,512,1296]{2,3,1,0:T(8,128)(2,1)S(1)}, bf16[1,1,512,1296]{2,3,1,0:T(8,128)(2,1)}, u32[]{:S(2)}) copy-start(bf16[1,1,512,1296]{2,3,1,0:T(8,128)(2,1)} %param.14) | copy-start | bytes 3981316
  0.0 10.1 %copy-start.15 = (s32[1,1,64,4,4]{2,4,3,1,0:T(4,128)S(1)}, s32[1,1,64,4,4]{2,4,3,1,0:T(4,128)}, u32[]{:S(2)}) copy-start(s32[1,1,64,4,4]{2,4,3,1,0:T(4,128)} %param.15) | copy-start | bytes 12292
  2.3 13.9 %collective-permute-start = (f32[82,3,512]{2,0,1:T(8,128)S(1)}, f32[82,3,512]{2,0,1:T(8,128)}, u32[]{:S(2)}, u32[]{:S(2)}) collective-permute-start(f32[82,3,512]{2,0,1:T(8,128)S(1)} %copy.18), channel_id=1, source_target_pairs={{1,0},{2,1},{3,2},{5,4},{6,5},{7,6},{9,8},{10,9},{11,10},{13,12},{... | collective-permute-start | bytes 1511432 | tf_op jit(solution)/shard_map/ppermute | solution.py:235
  4.6 13.7 %collective-permute-start.1 = (f32[82,3,512]{2,0,1:T(8,128)}, f32[82,3,512]{2,0,1:T(8,128)}, u32[]{:S(2)}, u32[]{:S(2)}) collective-permute-start(f32[82,3,512]{2,0,1:T(8,128)} %copy.19), channel_id=1, source_target_pairs={{0,1},{1,2},{2,3},{4,5},{5,6},{6,7},{8,9},{9,10},{10,11},{12,13},{... | collective-permute-start | bytes 1511432 | tf_op jit(solution)/shard_map/ppermute | solution.py:236
  10.4 10.1 %copy-start.14 = (f32[2,8,512]{2,1,0:T(8,128)S(1)}, f32[2,8,512]{2,1,0:T(8,128)}, u32[]{:S(2)}) copy-start(f32[2,8,512]{2,1,0:T(8,128)} %param.13) | copy-start | bytes 98308
  13.7 6.8 %copy-start.10 = (f32[5,16,8,512]{3,2,1,0:T(8,128)S(1)}, f32[5,16,8,512]{3,2,1,0:T(8,128)}, u32[]{:S(2)}) copy-start(f32[5,16,8,512]{3,2,1,0:T(8,128)} %param.12) | copy-start | bytes 3932164
  17.6 4.3 %copy-start.11 = (f32[82,3,512]{2,1,0:T(4,128)}, f32[82,3,512]{2,1,0:T(4,128)S(1)}, u32[]{:S(2)}) copy-start(f32[82,3,512]{2,1,0:T(4,128)S(1)} %copy.20) | copy-start | bytes 1511428
  19.7 0.8 copy-start.12
  20.5 1.3 copy-start.13
  23.3 105.3 %collective-permute-start.2 = (f32[82,16,3]{0,1,2:T(8,128)S(1)}, f32[82,16,3]{0,1,2:T(8,128)S(1)}, u32[]{:S(2)}, u32[]{:S(2)}) collective-permute-start(f32[82,16,3]{0,1,2:T(8,128)S(1)} %copy.22), channel_id=1, source_target_pairs={{4,0},{8,4},{12,8},{16,12},{20,16},{24,20},{28,24},{32,28},{36,32}... | collective-permute-start | bytes 47240 | tf_op jit(solution)/shard_map/ppermute | solution.py:238
  27.4 102.4 %collective-permute-start.3 = (f32[82,16,3]{0,1,2:T(8,128)S(1)}, f32[82,16,3]{0,1,2:T(8,128)S(1)}, u32[]{:S(2)}, u32[]{:S(2)}) collective-permute-start(f32[82,16,3]{0,1,2:T(8,128)S(1)} %copy.23), channel_id=1, source_target_pairs={{0,4},{4,8},{8,12},{12,16},{16,20},{20,24},{24,28},{28,32},{32,36}... | collective-permute-start | bytes 47240 | tf_op jit(solution)/shard_map/ppermute | solution.py:239
  40.2 4.4 %slice-start = ((bf16[256,4,1296]{2,1,0:T(4,128)(2,1)}), bf16[256,4,272]{2,1,0:T(4,128)(2,1)S(1)}, s32[]{:S(2)}) async-start(bf16[256,4,1296]{2,1,0:T(4,128)(2,1)} %reshape.49), calls=%async_computation | async-start | bytes 1572864 | tf_op jit(solution)/shard_map/slice | solution.py:259
  127.3 1.3 copy-start.1
  134.8 21.4 %copy-start.16 = (f32[2,72]{1,0:T(2,128)S(1)}, f32[2,72]{1,0:T(2,128)}, u32[]{:S(2)}) copy-start(f32[2,72]{1,0:T(2,128)} %pad_maximum_fusion.7) | copy-start | bytes 1732
  134.8 21.5 %copy-start.2 = (s32[4,8,512]{2,1,0:T(8,128)S(1)}, s32[4,8,512]{2,1,0:T(8,128)}, u32[]{:S(2)}) copy-start(s32[4,8,512]{2,1,0:T(8,128)} %slot.1) | copy-start | bytes 196612
  134.8 21.5 %copy-start.3 = (f32[4,8,512]{2,1,0:T(8,128)S(1)}, f32[4,8,512]{2,1,0:T(8,128)}, u32[]{:S(2)}) copy-start(f32[4,8,512]{2,1,0:T(8,128)} %weight.1) | copy-start | bytes 196612
  134.8 21.5 %copy-start.4 = (bf16[16,1296]{1,0:T(8,128)(2,1)S(1)}, bf16[16,1296]{1,0:T(8,128)(2,1)}, u32[]{:S(2)}) copy-start(bf16[16,1296]{1,0:T(8,128)(2,1)} %strain.1) | copy-start | bytes 124420
  134.8 21.5 %copy-start.5 = (f32[8,512]{1,0:T(8,128)S(1)}, f32[8,512]{1,0:T(8,128)}, u32[]{:S(2)}) copy-start(f32[8,512]{1,0:T(8,128)} %thick.1) | copy-start | bytes 49156
  134.9 21.5 %copy-start.6 = (f32[8,512]{1,0:T(8,128)S(1)}, f32[8,512]{1,0:T(8,128)}, u32[]{:S(2)}) copy-start(f32[8,512]{1,0:T(8,128)} %edge.1) | copy-start | bytes 49156
  134.9 21.5 %copy-start.7 = (s32[8,512]{1,0:T(8,128)S(1)}, s32[8,512]{1,0:T(8,128)}, u32[]{:S(2)}) copy-start(s32[8,512]{1,0:T(8,128)} %ice.1) | copy-start | bytes 49156
  134.9 21.5 %copy-start.8 = (s32[8,512]{1,0:T(8,128)S(1)}, s32[8,512]{1,0:T(8,128)}, u32[]{:S(2)}) copy-start(s32[8,512]{1,0:T(8,128)} %brk.1) | copy-start | bytes 49156
  134.9 21.5 %copy-start.9 = (f32[36]{0:T(128)S(1)}, f32[36]{0:T(128)}, u32[]{:S(2)}) copy-start(f32[36]{0:T(128)} %decay.1) | copy-start | bytes 436

commit v2 on v1

v2 whole, which is shorter than its diff:
```python
import functools
import math

import jax
import jax.numpy as jnp
import numpy as np
from jax import lax
from jax.experimental import pallas as pl
from jax.experimental.pallas import tpu as pltpu
from jax.sharding import PartitionSpec as P

MESH = pl.DeviceIdType.MESH
F32 = jnp.float32
BF16 = jnp.bfloat16
NDIR = 36
NBIN = 1296
NSUB = 3
N_DEV = 256
SPLIT = 1024
TAIL = 384
COLUMN_ROWS = 768


def coords():
    t, s = lax.axis_index("tiles"), lax.axis_index("sub")
    return t // 16, lax.rem(t, 16), s


def zc_peer(i, x, zc, s):
    c = lax.rem(lax.rem(zc, 2) + i % 2, 2)
    z = lax.rem(zc // 2 + i // 2, 8)
    return (x * 16 + z * 2 + c, s)


def xy_peer(i, x, zc, s):
    return (lax.rem(x + i // 4, 4) * 16 + zc, lax.rem(s + i % 4, 4))


def tile_of(x, zc, dx, dz, dc):
    core = lax.rem(lax.rem(zc, 2) + dc, 2)
    return lax.rem(x + dx, 4) * 16 + lax.rem(zc // 2 + dz, 8) * 2 + core


def send_all(src, dst, send_sem, recv_sem):
    x, zc, s = coords()
    me = (x * 16 + zc) * 4 + s

    def one(i, carry):
        tile = tile_of(x, zc, i // 64, lax.rem(i // 2, 8), lax.rem(i, 2))
        sub = lax.rem(s + lax.rem(i // 16, 4), 4)
        pltpu.make_async_remote_copy(
            src_ref=src.at[tile * 4 + sub],
            dst_ref=dst.at[me],
            send_sem=send_sem,
            recv_sem=recv_sem,
            device_id=(tile, sub),
            device_id_type=MESH,
        ).start()
        return carry

    lax.fori_loop(1, N_DEV, one, 0)


def gather_rows(picks, spectra, xa, xb):
    pick = picks[...].astype(F32).reshape(N_DEV, 1, 4)
    pick = jnp.broadcast_to(pick, (N_DEV, 4, 4)).reshape(N_DEV * 4, 4)
    row = lax.broadcasted_iota(jnp.int32, (N_DEV * 4, 4), 0)
    lane = lax.broadcasted_iota(jnp.int32, (N_DEV * 4, 4), 1)
    column = jnp.sum(jnp.where(lane == lax.rem(row, 4), pick, 0.0), axis=1, keepdims=True)
    column = column.astype(jnp.int32)
    cell = lax.broadcasted_iota(jnp.int32, (256, 512), 1)
    for b in range(4):
        choose = jnp.where(cell == column[b * 256 : b * 256 + 256], 1.0, 0.0).astype(BF16)
        rows = jnp.dot(choose, spectra[...], preferred_element_type=F32).astype(BF16)
        devices = pl.ds(b * 64, 64)
        xa[devices] = rows[:, :SPLIT].reshape(64, 4, SPLIT)
        rest = jnp.concatenate(
            [rows[:, SPLIT:], jnp.zeros((256, SPLIT + TAIL - NBIN), BF16)], axis=1
        )
        xb[devices] = rest.reshape(64, 4, TAIL)


def pack_halo(floe, courant, row_send, col_send):
    for n in range(5):
        row_send[0, n * 16 : n * 16 + 16] = floe[n, :, 0:4, :]
        row_send[1, n * 16 : n * 16 + 16] = floe[n, :, 4:8, :]
    row_send[0, 80:82] = courant[:, 0:4, :]
    row_send[1, 80:82] = courant[:, 4:8, :]
    filler = jnp.zeros((COLUMN_ROWS - 656, 128), F32)
    for side, lanes in ((0, slice(0, 128)), (1, slice(384, 512))):
        strip = jnp.concatenate(
            [floe[:, :, :, lanes].reshape(640, 128), courant[:, :, lanes].reshape(16, 128), filler]
        )
        turned = strip.T
        col_send[side] = turned[0:8] if side == 0 else turned[120:128]


def halo_copies(row_send, row_recv, col_send, col_recv, send_sem, recv_sem):
    t, s = lax.axis_index("tiles"), lax.axis_index("sub")
    n_tiles = lax.axis_size("tiles")
    copies = []

    def add(src, dst, device):
        k = len(copies)
        copies.append(
            pltpu.make_async_remote_copy(
                src_ref=src,
                dst_ref=dst,
                send_sem=send_sem.at[k],
                recv_sem=recv_sem.at[k],
                device_id=device,
                device_id_type=MESH,
            )
        )

    for side, step in ((0, n_tiles - 1), (1, 1)):
        for group, shift in ((0, 0), (1, 3), (2, 1)):
            device = (lax.rem(t + step, n_tiles), lax.rem(s + shift, 4))
            add(col_send.at[side], col_recv.at[side, group], device)
    add(row_send.at[0], row_recv.at[0], (t, lax.rem(s + 3, 4)))
    add(row_send.at[1], row_recv.at[1], (t, lax.rem(s + 1, 4)))
    return copies


def unpack_columns(col_recv, side):
    for group in range(3):
        side[group] = jnp.concatenate(
            [col_recv[0, group], jnp.zeros((112, COLUMN_ROWS), F32), col_recv[1, group]], axis=0
        ).T


def transport(floe, courant, row_recv, side, out):
    s = lax.axis_index("sub")
    row = lax.broadcasted_iota(jnp.int32, (8, 128), 0)

    def frame(own, layer):
        start = layer * 8 if isinstance(layer, int) else pl.multiple_of(layer * 8, 8)
        here = pl.ds(start, 8)
        corner = jnp.where(row < 4, side[1, here], side[2, here])
        top = jnp.concatenate([own, side[0, here]], axis=1)
        halo = jnp.concatenate([row_recv[0, layer], row_recv[1, layer]], axis=0)
        return top, jnp.concatenate([halo, corner], axis=1)

    wide_row = lax.broadcasted_iota(jnp.int32, (8, 640), 0)
    after, before = jnp.where(s < 3, 1.0, 0.0), jnp.where(s > 0, 1.0, 0.0)
    inside = jnp.where(wide_row < 4, after, before)
    parts = []
    for k in range(2):
        top, halo = frame(courant[k], 80 + k)
        parts.append(jnp.concatenate([top, halo * inside], axis=0))
    east, west = jnp.maximum(parts[0], 0.0), jnp.maximum(-parts[0], 0.0)
    north, south = jnp.maximum(parts[1], 0.0), jnp.maximum(-parts[1], 0.0)
    keep = 1.0 - east - west - north - south

    def one(layer):
        n, k = layer // 16, lax.rem(layer, 16)
        v = jnp.concatenate(frame(floe[n, k], layer), axis=0)
        for _ in range(NSUB):
            v = (
                v * keep
                + pltpu.roll(v * east, 1, 1)
                + pltpu.roll(v * west, 639, 1)
                + pltpu.roll(v * north, 1, 0)
                + pltpu.roll(v * south, 15, 0)
            )
        out[n, k] = v[0:8, 0:512]

    def pair(i, carry):
        one(2 * i)
        one(2 * i + 1)
        return carry

    lax.fori_loop(0, 40, pair, 0)


def transpose_in(src, table, first, width):
    for lane in range(0, width, 128):
        size = min(128, width - lane)
        block = src[:, :, lane : lane + 128].reshape(N_DEV * 4, 128)
        turned = block.T
        table[first + lane : first + lane + size, :] = turned[:size]


def build_mixing(r, slot, weight, mixing):
    rows = lax.broadcasted_iota(jnp.int32, (N_DEV * 4, 512), 0).astype(jnp.int16)
    total = jnp.zeros((N_DEV * 4, 512), BF16)
    for k in range(4):
        slots = slot[k, pl.ds(r, 1), :].astype(jnp.int16)
        weights = weight[k, pl.ds(r, 1), :].astype(BF16)
        total = total + jnp.where(rows == slots, weights, jnp.zeros((), BF16))
    mixing[r] = total


def wide(column, lanes=4):
    return jnp.concatenate([column] * lanes, axis=1)


def fill_decay(decay, decay_table):
    row = lax.broadcasted_iota(jnp.int32, (72, 128), 0)
    for g in range(18):
        decay_table[g * 72 : g * 72 + 72, :] = jnp.where(row < 36, decay[2 * g], decay[2 * g + 1])


def fill_paths(thick, edge, trig, paths):
    cos_edge, sin_edge = jnp.cos(edge[...]), jnp.sin(edge[...])
    scaled = -math.log2(math.e) * thick[...]
    for r in range(8):
        cosine = wide(trig[0]) * cos_edge[r : r + 1] + wide(trig[1]) * sin_edge[r : r + 1]
        paths[r] = scaled[r : r + 1] / (0.25 + 0.75 * cosine * cosine)


def attenuate(r, steps, table, mixing, decay_table, paths, att):
    path = paths[r]
    for start, size in steps:
        spectrum = jnp.dot(table[start : start + size, :], mixing[r], preferred_element_type=F32)
        decay_rows = wide(decay_table[start : start + size, :])
        first = start % 72
        pieces, have = [path[first:]], 72 - first
        while have < size:
            pieces.append(path)
            have += 72
        factor = jnp.concatenate(pieces, axis=0)[:size]
        att[start : start + size, :] = (spectrum * jnp.exp2(decay_rows * factor)).astype(BF16)


def fracture(hist, weight, ice, brk, out):
    total_w = weight[0] + weight[1] + weight[2] + weight[3]
    used_w = sum(weight[k].astype(BF16).astype(F32) for k in range(4))
    fix = total_w / used_w
    rows = [hist[j] * fix for j in range(16)]
    total = functools.reduce(jnp.add, rows)
    strength = ice[...].astype(F32) * total / (total + 0.005 * 16 * NBIN)
    scale = strength / total
    share = [v * scale for v in rows]
    shorter, run = [], jnp.zeros_like(total)
    for j in range(16):
        shorter.append(run)
        run = run + share[j]
    brk_rows = brk[...]
    for n in range(5):
        above = jnp.zeros_like(total)
        for k in range(15, -1, -1):
            value = out[n, k]
            breakable = jnp.where(brk_rows <= k, value, 0.0)
            out[n, k] = value - breakable * shorter[k] + above * share[k]
            above = above + breakable


STEPS_A = [(i * 144, 144) for i in range(6)] + [(864, 160)]
STEPS_B = [(1024, 128), (1152, 144)]


def kernel(
    decay, floe, courant, spectra, picks, slot, weight, thick, edge, strain, ice, brk, trig, out,
    xa, xb, ra, rb, row_send, row_recv, col_send, col_recv, side,
    table, mixing, decay_table, paths, att, hist,
    send_sem, recv_sem, own_sem, halo_send, halo_recv, group_sem
):
    x, zc, s = coords()
    me = (x * 16 + zc) * 4 + s
    barrier = pltpu.get_barrier_semaphore()
    for i in range(1, 16):
        pl.semaphore_signal(barrier, inc=1, device_id=zc_peer(i, x, zc, s), device_id_type=MESH)
        pl.semaphore_signal(barrier, inc=1, device_id=xy_peer(i, x, zc, s), device_id_type=MESH)
    gather_rows(picks, spectra, xa, xb)
    pl.semaphore_wait(barrier, 30)
    for i in range(1, 16):
        pl.semaphore_signal(group_sem, inc=1, device_id=xy_peer(i, x, zc, s), device_id_type=MESH)
    pack_halo(floe, courant, row_send, col_send)
    pl.semaphore_wait(group_sem, 15)

    halo = halo_copies(row_send, row_recv, col_send, col_recv, halo_send, halo_recv)
    for copy in halo:
        copy.start()
    own = [
        pltpu.make_async_copy(xa.at[me], ra.at[me], own_sem.at[0]),
        pltpu.make_async_copy(xb.at[me], rb.at[me], own_sem.at[1]),
    ]
    for copy in own:
        copy.start()
    send_all(xa, ra, send_sem.at[0], recv_sem.at[0])
    send_all(xb, rb, send_sem.at[1], recv_sem.at[1])

    fill_decay(decay, decay_table)
    fill_paths(thick, edge, trig, paths)

    def mix_row(r, carry):
        build_mixing(r, slot, weight, mixing)
        return carry

    lax.fori_loop(0, 8, mix_row, 0)
    for copy in halo:
        copy.wait()
    unpack_columns(col_recv, side)
    transport(floe, courant, row_recv, side, out)

    others = pl.ds(0, N_DEV - 1)
    own[0].wait()
    pltpu.make_async_copy(xa.at[others], ra.at[others], recv_sem.at[0]).wait()
    transpose_in(ra, table, 0, SPLIT)

    def row_a(r, carry):
        attenuate(r, STEPS_A, table, mixing, decay_table, paths, att)
        part = jnp.dot(strain[:, :SPLIT], att[:SPLIT], preferred_element_type=F32)
        hist[:, pl.ds(r, 1), :] = part[:, None, :]
        return carry

    lax.fori_loop(0, 8, row_a, 0)
    own[1].wait()
    pltpu.make_async_copy(xb.at[others], rb.at[others], recv_sem.at[1]).wait()
    transpose_in(rb, table, SPLIT, NBIN - SPLIT)

    def row_b(r, carry):
        attenuate(r, STEPS_B, table, mixing, decay_table, paths, att)
        part = jnp.dot(strain[:, SPLIT:], att[SPLIT:], preferred_element_type=F32)
        hist[:, pl.ds(r, 1), :] += part[:, None, :]
        return carry

    lax.fori_loop(0, 8, row_b, 0)
    fracture(hist, weight, ice, brk, out)
    pltpu.make_async_copy(xa.at[others], ra.at[others], send_sem.at[0]).wait()
    pltpu.make_async_copy(xb.at[others], rb.at[others], send_sem.at[1]).wait()


def shards(
    floe_area, courant, spectra, send_rows, src_slot, src_weight, thickness, edge_angle,
    decay_rate, strain_table, ice_mask, break_bin
):
    angles = 2.0 * math.pi * np.tile(np.arange(NDIR), 2) / NDIR - math.pi
    trig = np.stack([np.cos(angles), np.sin(angles)]).astype(np.float32)
    trig = jnp.asarray(np.broadcast_to(trig[:, :, None], (2, 72, 128)))
    vmem = pl.BlockSpec(memory_space=pltpu.VMEM)
    return pl.pallas_call(
        kernel,
        out_shape=jax.ShapeDtypeStruct(floe_area.shape, F32),
        in_specs=[pl.BlockSpec(memory_space=pltpu.SMEM)] + [vmem] * 12,
        out_specs=vmem,
        scratch_shapes=[
            pltpu.VMEM((N_DEV, 4, SPLIT), BF16),
            pltpu.VMEM((N_DEV, 4, TAIL), BF16),
            pltpu.VMEM((N_DEV, 4, SPLIT), BF16),
            pltpu.VMEM((N_DEV, 4, TAIL), BF16),
            pltpu.VMEM((2, 82, 4, 512), F32),
            pltpu.VMEM((2, 82, 4, 512), F32),
            pltpu.VMEM((2, 8, COLUMN_ROWS), F32),
            pltpu.VMEM((2, 3, 8, COLUMN_ROWS), F32),
            pltpu.VMEM((3, COLUMN_ROWS, 128), F32),
            pltpu.VMEM((NBIN, N_DEV * 4), BF16),
            pltpu.VMEM((8, N_DEV * 4, 512), BF16),
            pltpu.VMEM((NBIN, 128), F32),
            pltpu.VMEM((8, 72, 512), F32),
            pltpu.VMEM((NBIN, 512), BF16),
            pltpu.VMEM((16, 8, 512), F32),
            pltpu.SemaphoreType.DMA((2,)),
            pltpu.SemaphoreType.DMA((2,)),
            pltpu.SemaphoreType.DMA((2,)),
            pltpu.SemaphoreType.DMA((8,)),
            pltpu.SemaphoreType.DMA((8,)),
            pltpu.SemaphoreType.REGULAR,
        ],
        compiler_params=pltpu.CompilerParams(
            collective_id=0, has_side_effects=True, vmem_limit_bytes=56 << 20
        ),
    )(
        decay_rate, floe_area, courant, spectra[0, 0], send_rows[0, 0], src_slot, src_weight,
        thickness, edge_angle, strain_table, ice_mask, break_bin, trig
    )


def solution(mesh):
    in_specs = (
        P(None, None, "sub", "tiles"),
        P(None, "sub", "tiles"),
        P("tiles", "sub", None, None),
        P("tiles", "sub", None, None, None),
        P(None, "sub", "tiles"),
        P(None, "sub", "tiles"),
        P("sub", "tiles"),
        P("sub", "tiles"),
        P(),
        P(),
        P("sub", "tiles"),
        P("sub", "tiles"),
    )
    out_specs = P(None, None, "sub", "tiles")
    return jax.shard_map(shards, mesh=mesh, in_specs=in_specs, out_specs=out_specs, check_vma=False)
```

time: 177 us -> 95.4 us (0.54)
  Pallas kernels: 124 us -> 88 us
  local copies, waits for them, and re-layouts: 25.6 us -> 7.23 us
  starting transfers between devices: 12.5 us -> 0 us
  other arithmetic: 7.95 us -> 0 us
  matrix products: 3.25 us -> 0 us
  waiting for transfers between devices: 3.17 us -> 0 us
    pallas_call x3 -> x1, Pallas kernels: 124 us -> 88 us  [shards(): pl.pallas_call(kernel, out_shape=jax.ShapeDtypeStruct(floe_area.shape, F3...]
    ppermute x4 -> x0, starting transfers between devices: 12.5 us -> none  [the longest x1 5.47 us: transport(): lax.ppermute(joined[:, 5:8], 'sub', [(i, i + 1) for i in range(n_sub - 1)])]
    slice x7 -> x0, local copies, waits for them, and re-layouts: 6.57 us -> none  [the longest x1 3.72 us: shards(): ra, rb = exchange(outgoing[:, :, :SPLIT], tail)]
    concatenate x2 -> x0, other arithmetic: 5.97 us -> none  [the longest x1 3.82 us: transport(): jnp.concatenate([rows, right, jnp.zeros((82, 16, 122), F32), left], axis=2)]
    reshape x1 -> x0, local copies, waits for them, and re-layouts: 5.74 us -> none  [shards(): outgoing = outgoing.reshape(N_DEV, 4, NBIN)]
    ppermute x4 -> x0, local copies, waits for them, and re-layouts: 5.18 us -> none  [the longest x1 1.39 us: transport(): lax.ppermute(joined[:, 0:3], 'sub', [(i + 1, i) for i in range(n_sub - 1)])]
    convert_element_type x1 -> x0, local copies, waits for them, and re-layouts: 4.52 us -> none  [shards(): jnp.dot(choose, spectra[0, 0], preferred_element_type=F32).astype(BF16)]
    unnamed x35 -> x5, local copies, waits for them, and re-layouts: 2.27 us -> 6.52 us
  transfers between devices with their start and end apart: 4 -> 0, of which waited for: 2 -> 0; matrix products, arithmetic and copies ran while one was open for 13% -> 0% of each run, Pallas kernels for 47% -> 0%
where the time goes in v2:
time: 95.4 us; the launch traced here: 95.2 us
  Pallas kernels  88 us (92%)
  local copies, waits for them, and re-layouts  7.23 us (8%)
    pallas_call x1, Pallas kernels, shards(): pl.pallas_call(kernel, out_shape=jax.ShapeDtypeStruct(floe_area.shape, F3...  88 us
    unnamed x5, local copies, waits for them, and re-layouts  6.52 us

profile of v2, /device:TPU:1, one launch (start us, length us, event | category | flops | bytes accessed | tf_op | source)
XLA Modules:
  0.0 95.2 jit_solution(7583570177051495410)
XLA Ops:
  0.0 1.5 %copy.15 = s32[1,1,64,4,4]{4,3,2,1,0:T(4,128)} copy(s32[1,1,64,4,4]{2,4,3,1,0:T(4,128)} %param.16) | data formatting | bytes 8192 | tf_op args[3]
  1.5 0.0 copy-start
  1.5 2.5 %copy.14 = bf16[1,1,512,1296]{3,2,1,0:T(8,128)(2,1)} copy(bf16[1,1,512,1296]{2,3,1,0:T(8,128)(2,1)} %param.15) | data formatting | bytes 2654208 | tf_op args[2]
  4.0 0.0 copy-done
  4.0 0.7 jit_solution_.3.trig
  4.7 88.0 %shard_map.127 = f32[5,16,8,512]{3,2,1,0:T(8,128)} custom-call(f32[36]{0:T(128)} %decay.1, f32[5,16,8,512]{3,2,1,0:T(8,128)} %floe.1, f32[2,8,512]{2,1,0:T(8,128)} %courant.1, bf16[512,1296]{1,0:T(8,128)(2,1)} %bitcast.2, s32[64,4,4]{2,1,0:T(4,128)} %bitcast.3, s32[4,8,512]{2,1,0:T(8,128)} %slot.1, f32[4,8,512]{2,1,0:T(8,128)} %weight.1, f32[8,512]{1,0:T(8,128)} %thick.1, ...), custom_call_target="tpu_custom_call" | custom-call | tf_op jit(solution)/shard_map/pallas_call | solution.py:333
  92.7 2.5 %copy.17 = f32[5,16,8,512]{3,2,1,0:T(8,128)} copy(f32[5,16,8,512]{3,2,1,0:T(8,128)} %shard_map.127) | data formatting | bytes 2621440
Async XLA Ops:
  1.5 2.5 %copy-start = (f32[2,72]{1,0:T(2,128)S(1)}, f32[2,72]{1,0:T(2,128)}, u32[]{:S(2)}) copy-start(f32[2,72]{1,0:T(2,128)} %constant.2.clone) | copy-start | bytes 1732

commit v3 on v2

--- a/solution.py
+++ b/solution.py
@@ -3,7 +3,6 @@
 
 import jax
 import jax.numpy as jnp
-import numpy as np
 from jax import lax
 from jax.experimental import pallas as pl
 from jax.experimental.pallas import tpu as pltpu
@@ -17,7 +16,8 @@
 NSUB = 3
 N_DEV = 256
 SPLIT = 1024
-TAIL = 384
+TAIL = 256
+WIDE = SPLIT + TAIL
 COLUMN_ROWS = 768
 
 
@@ -43,7 +43,7 @@
 
 def send_all(src, dst, send_sem, recv_sem):
     x, zc, s = coords()
-    me = (x * 16 + zc) * 4 + s
+    me = (zc * 4 + x) * 4 + s
 
     def one(i, carry):
         tile = tile_of(x, zc, i // 64, lax.rem(i // 2, 8), lax.rem(i, 2))
@@ -61,23 +61,63 @@
     lax.fori_loop(1, N_DEV, one, 0)
 
 
-def gather_rows(picks, spectra, xa, xb):
-    pick = picks[...].astype(F32).reshape(N_DEV, 1, 4)
-    pick = jnp.broadcast_to(pick, (N_DEV, 4, 4)).reshape(N_DEV * 4, 4)
-    row = lax.broadcasted_iota(jnp.int32, (N_DEV * 4, 4), 0)
-    lane = lax.broadcasted_iota(jnp.int32, (N_DEV * 4, 4), 1)
-    column = jnp.sum(jnp.where(lane == lax.rem(row, 4), pick, 0.0), axis=1, keepdims=True)
-    column = column.astype(jnp.int32)
-    cell = lax.broadcasted_iota(jnp.int32, (256, 512), 1)
-    for b in range(4):
-        choose = jnp.where(cell == column[b * 256 : b * 256 + 256], 1.0, 0.0).astype(BF16)
-        rows = jnp.dot(choose, spectra[...], preferred_element_type=F32).astype(BF16)
-        devices = pl.ds(b * 64, 64)
-        xa[devices] = rows[:, :SPLIT].reshape(64, 4, SPLIT)
-        rest = jnp.concatenate(
-            [rows[:, SPLIT:], jnp.zeros((256, SPLIT + TAIL - NBIN), BF16)], axis=1
+def send_group(peer, number, src, dst, me, send_sem, recv_sem):
+    x, zc, s = coords()
+    for i in range(1, 16):
+        device = peer(i, x, zc, s)
+        pltpu.make_async_remote_copy(
+            src_ref=src.at[number(device)],
+            dst_ref=dst.at[me],
+            send_sem=send_sem,
+            recv_sem=recv_sem,
+            device_id=device,
+            device_id_type=MESH,
+        ).start()
+
+
+def choose_cells(picks, choose):
+    pick = picks[...].reshape(16, 64).astype(F32)
+    pick = jnp.concatenate([pick, jnp.zeros((16, 64), F32)], axis=1).T[:64]
+    pick = jnp.broadcast_to(pick.reshape(64, 1, 16), (64, 16, 16)).reshape(N_DEV * 4, 16)
+    row = lax.broadcasted_iota(jnp.int32, (N_DEV * 4, 16), 0)
+    lane = lax.broadcasted_iota(jnp.int32, (N_DEV * 4, 16), 1)
+    column = jnp.sum(jnp.where(lane == lax.rem(row, 16), pick, 0.0), axis=1, keepdims=True)
+    cell = lax.broadcasted_iota(jnp.int32, (N_DEV * 4, 512), 1)
+    choose[...] = jnp.where(cell == column.astype(jnp.int32), 1.0, 0.0).astype(BF16)
+
+
+def gather_rows(choose, spectra, xa, xb, tail_send):
+    over_cells = (((1,), (1,)), ((), ()))
+    for start in range(0, WIDE, 256):
+        rows = lax.dot_general(
+            choose[...], spectra[start : start + 256, :], over_cells, preferred_element_type=F32
         )
-        xb[devices] = rest.reshape(64, 4, TAIL)
+        rows = rows.astype(BF16).reshape(N_DEV, 4, 256)
+        if start < SPLIT:
+            xa[:, :, start : start + 256] = rows
+        else:
+            xb[...] = rows
+    last = lax.dot_general(
+        choose[...], spectra[WIDE:, :], over_cells, preferred_element_type=F32
+    )
+    filler = jnp.zeros((64, NBIN - WIDE), F32)
+    for zc in range(16):
+        pieces = [last[(x * 16 + zc) * 16 : (x * 16 + zc) * 16 + 16] for x in range(4)]
+        tail_send[zc] = jnp.concatenate(pieces + [filler], axis=0).T.astype(BF16)
+
+
+def regroup_tail(tail_mid, tail_pass):
+    turned = tail_mid[...].reshape(256, 128).T
+    tail_pass[...] = turned[:64].reshape(16, 4, 256)
+
+
+def finish_tail(tail_recv, table):
+    turned = tail_recv[...].reshape(64, 256).T
+    for zc in range(0, 16, 2):
+        both = jnp.concatenate(
+            [turned[zc * 16 : zc * 16 + 16], turned[zc * 16 + 16 : zc * 16 + 32]], axis=1
+        )
+        table[WIDE:, zc * 64 : zc * 64 + 128] = both
 
 
 def pack_halo(floe, courant, row_send, col_send):
@@ -185,7 +225,9 @@
     rows = lax.broadcasted_iota(jnp.int32, (N_DEV * 4, 512), 0).astype(jnp.int16)
     total = jnp.zeros((N_DEV * 4, 512), BF16)
     for k in range(4):
-        slots = slot[k, pl.ds(r, 1), :].astype(jnp.int16)
+        given = slot[k, pl.ds(r, 1), :]
+        slots = lax.rem(given // 16, 16) * 64 + given // 256 * 16 + lax.rem(given, 16)
+        slots = slots.astype(jnp.int16)
         weights = weight[k, pl.ds(r, 1), :].astype(BF16)
         total = total + jnp.where(rows == slots, weights, jnp.zeros((), BF16))
     mixing[r] = total
@@ -201,7 +243,10 @@
         decay_table[g * 72 : g * 72 + 72, :] = jnp.where(row < 36, decay[2 * g], decay[2 * g + 1])
 
 
-def fill_paths(thick, edge, trig, paths):
+def fill_paths(thick, edge, paths):
+    direction = lax.rem(lax.broadcasted_iota(jnp.int32, (72, 128), 0), NDIR).astype(F32)
+    angle = 2.0 * math.pi * direction / NDIR - math.pi
+    trig = (jnp.cos(angle), jnp.sin(angle))
     cos_edge, sin_edge = jnp.cos(edge[...]), jnp.sin(edge[...])
     scaled = -math.log2(math.e) * thick[...]
     for r in range(8):
@@ -251,38 +296,75 @@
 
 
 def kernel(
-    decay, floe, courant, spectra, picks, slot, weight, thick, edge, strain, ice, brk, trig, out,
-    xa, xb, ra, rb, row_send, row_recv, col_send, col_recv, side,
+    decay, floe_hbm, courant_hbm, spectra_hbm, picks_hbm, slot_hbm, weight_hbm, thick_hbm, edge_hbm,
+    strain_hbm, ice_hbm, brk_hbm, out,
+    floe, courant, spectra, picks, slot, weight, thick, edge, strain, ice, brk,
+    choose, xa, xb, ra, rb, tail_send, tail_mid, tail_pass, tail_recv,
+    row_send, row_recv, col_send, col_recv, side,
     table, mixing, decay_table, paths, att, hist,
-    send_sem, recv_sem, own_sem, halo_send, halo_recv, group_sem
+    load_sem, send_sem, recv_sem, own_sem, halo_send, halo_recv, group_sem
 ):
     x, zc, s = coords()
     me = (x * 16 + zc) * 4 + s
+    me_slot = (zc * 4 + x) * 4 + s
     barrier = pltpu.get_barrier_semaphore()
     for i in range(1, 16):
         pl.semaphore_signal(barrier, inc=1, device_id=zc_peer(i, x, zc, s), device_id_type=MESH)
         pl.semaphore_signal(barrier, inc=1, device_id=xy_peer(i, x, zc, s), device_id_type=MESH)
-    gather_rows(picks, spectra, xa, xb)
+    pairs = (
+        (picks_hbm, picks), (spectra_hbm, spectra), (floe_hbm, floe), (courant_hbm, courant),
+        (slot_hbm, slot), (weight_hbm, weight), (thick_hbm, thick), (edge_hbm, edge),
+        (strain_hbm, strain), (ice_hbm, ice), (brk_hbm, brk),
+    )
+    loads = [
+        pltpu.make_async_copy(src, dst, load_sem.at[k]) for k, (src, dst) in enumerate(pairs)
+    ]
+    for copy in loads:
+        copy.start()
+    loads[0].wait()
+    choose_cells(picks, choose)
     pl.semaphore_wait(barrier, 30)
     for i in range(1, 16):
         pl.semaphore_signal(group_sem, inc=1, device_id=xy_peer(i, x, zc, s), device_id_type=MESH)
+    loads[1].wait()
+    gather_rows(choose, spectra, xa, xb, tail_send)
+    for copy in loads[2:]:
+        copy.wait()
     pack_halo(floe, courant, row_send, col_send)
     pl.semaphore_wait(group_sem, 15)
+
+    def zc_number(device):
+        return lax.rem(device[0], 16)
+
+    def xy_number(device):
+        return device[0] // 16 * 4 + device[1]
 
     halo = halo_copies(row_send, row_recv, col_send, col_recv, halo_send, halo_recv)
     for copy in halo:
         copy.start()
     own = [
-        pltpu.make_async_copy(xa.at[me], ra.at[me], own_sem.at[0]),
-        pltpu.make_async_copy(xb.at[me], rb.at[me], own_sem.at[1]),
+        pltpu.make_async_copy(xa.at[me], ra.at[me_slot], own_sem.at[0]),
+        pltpu.make_async_copy(xb.at[me], rb.at[me_slot], own_sem.at[1]),
+        pltpu.make_async_copy(tail_send.at[zc], tail_mid.at[zc], own_sem.at[2]),
     ]
     for copy in own:
         copy.start()
+    send_group(zc_peer, zc_number, tail_send, tail_mid, zc, send_sem.at[2], recv_sem.at[2])
     send_all(xa, ra, send_sem.at[0], recv_sem.at[0])
     send_all(xb, rb, send_sem.at[1], recv_sem.at[1])
 
+    fifteen = pl.ds(0, 15)
+    own[2].wait()
+    pltpu.make_async_copy(tail_send.at[fifteen], tail_mid.at[fifteen], recv_sem.at[2]).wait()
+    regroup_tail(tail_mid, tail_pass)
+    own_tail = pltpu.make_async_copy(
+        tail_pass.at[x * 4 + s], tail_recv.at[x * 4 + s], own_sem.at[3]
+    )
+    own_tail.start()
+    send_group(xy_peer, xy_number, tail_pass, tail_recv, x * 4 + s, send_sem.at[3], recv_sem.at[3])
+
     fill_decay(decay, decay_table)
-    fill_paths(thick, edge, trig, paths)
+    fill_paths(thick, edge, paths)
 
     def mix_row(r, carry):
         build_mixing(r, slot, weight, mixing)
@@ -294,6 +376,10 @@
     unpack_columns(col_recv, side)
     transport(floe, courant, row_recv, side, out)
 
+    own_tail.wait()
+    pltpu.make_async_copy(tail_pass.at[fifteen], tail_recv.at[fifteen], recv_sem.at[3]).wait()
+    finish_tail(tail_recv, table)
+
     others = pl.ds(0, N_DEV - 1)
     own[0].wait()
     pltpu.make_async_copy(xa.at[others], ra.at[others], recv_sem.at[0]).wait()
@@ -308,7 +394,7 @@
     lax.fori_loop(0, 8, row_a, 0)
     own[1].wait()
     pltpu.make_async_copy(xb.at[others], rb.at[others], recv_sem.at[1]).wait()
-    transpose_in(rb, table, SPLIT, NBIN - SPLIT)
+    transpose_in(rb, table, SPLIT, TAIL)
 
     def row_b(r, carry):
         attenuate(r, STEPS_B, table, mixing, decay_table, paths, att)
@@ -320,26 +406,36 @@
     fracture(hist, weight, ice, brk, out)
     pltpu.make_async_copy(xa.at[others], ra.at[others], send_sem.at[0]).wait()
     pltpu.make_async_copy(xb.at[others], rb.at[others], send_sem.at[1]).wait()
+    pltpu.make_async_copy(tail_send.at[fifteen], tail_mid.at[fifteen], send_sem.at[2]).wait()
+    pltpu.make_async_copy(tail_pass.at[fifteen], tail_recv.at[fifteen], send_sem.at[3]).wait()
 
 
 def shards(
     floe_area, courant, spectra, send_rows, src_slot, src_weight, thickness, edge_angle,
     decay_rate, strain_table, ice_mask, break_bin
 ):
-    angles = 2.0 * math.pi * np.tile(np.arange(NDIR), 2) / NDIR - math.pi
-    trig = np.stack([np.cos(angles), np.sin(angles)]).astype(np.float32)
-    trig = jnp.asarray(np.broadcast_to(trig[:, :, None], (2, 72, 128)))
+    operands = (
+        floe_area, courant, spectra[0, 0].T, jnp.transpose(send_rows[0, 0], (1, 2, 0)), src_slot,
+        src_weight, thickness, edge_angle, strain_table, ice_mask, break_bin
+    )
     vmem = pl.BlockSpec(memory_space=pltpu.VMEM)
     return pl.pallas_call(
         kernel,
         out_shape=jax.ShapeDtypeStruct(floe_area.shape, F32),
-        in_specs=[pl.BlockSpec(memory_space=pltpu.SMEM)] + [vmem] * 12,
+        in_specs=[pl.BlockSpec(memory_space=pltpu.SMEM)]
+        + [pl.BlockSpec(memory_space=pl.ANY)] * len(operands),
         out_specs=vmem,
-        scratch_shapes=[
+        scratch_shapes=[pltpu.VMEM(v.shape, v.dtype) for v in operands]
+        + [
+            pltpu.VMEM((N_DEV * 4, 512), BF16),
             pltpu.VMEM((N_DEV, 4, SPLIT), BF16),
             pltpu.VMEM((N_DEV, 4, TAIL), BF16),
             pltpu.VMEM((N_DEV, 4, SPLIT), BF16),
             pltpu.VMEM((N_DEV, 4, TAIL), BF16),
+            pltpu.VMEM((16, 16, 128), BF16),
+            pltpu.VMEM((16, 16, 128), BF16),
+            pltpu.VMEM((16, 4, 256), BF16),
+            pltpu.VMEM((16, 4, 256), BF16),
             pltpu.VMEM((2, 82, 4, 512), F32),
             pltpu.VMEM((2, 82, 4, 512), F32),
             pltpu.VMEM((2, 8, COLUMN_ROWS), F32),
@@ -351,9 +447,10 @@
             pltpu.VMEM((8, 72, 512), F32),
             pltpu.VMEM((NBIN, 512), BF16),
             pltpu.VMEM((16, 8, 512), F32),
-            pltpu.SemaphoreType.DMA((2,)),
-            pltpu.SemaphoreType.DMA((2,)),
-            pltpu.SemaphoreType.DMA((2,)),
+            pltpu.SemaphoreType.DMA((len(operands),)),
+            pltpu.SemaphoreType.DMA((4,)),
+            pltpu.SemaphoreType.DMA((4,)),
+            pltpu.SemaphoreType.DMA((4,)),
             pltpu.SemaphoreType.DMA((8,)),
             pltpu.SemaphoreType.DMA((8,)),
             pltpu.SemaphoreType.REGULAR,
@@ -361,10 +458,7 @@
         compiler_params=pltpu.CompilerParams(
             collective_id=0, has_side_effects=True, vmem_limit_bytes=56 << 20
         ),
-    )(
-        decay_rate, floe_area, courant, spectra[0, 0], send_rows[0, 0], src_slot, src_weight,
-        thickness, edge_angle, strain_table, ice_mask, break_bin, trig
-    )
+    )(decay_rate, *operands)
 
 
 def solution(mesh):

time: 95.4 us -> 89 us (0.933)
  local copies, waits for them, and re-layouts: 7.23 us -> 2.52 us
  Pallas kernels: 88 us -> 86.3 us
    unnamed x5 -> x1, local copies, waits for them, and re-layouts: 6.52 us -> 2.52 us
    pallas_call x1, Pallas kernels: 88 us -> 86.3 us  [shards(): pl.pallas_call(kernel, out_shape=jax.ShapeDtypeStruct(floe_area.shape, F3...]
where the time goes in v3:
time: 89 us; the launch traced here: 88.9 us
  Pallas kernels  86.3 us (97%)
  local copies, waits for them, and re-layouts  2.52 us (3%)
    pallas_call x1, Pallas kernels, shards(): pl.pallas_call(kernel, out_shape=jax.ShapeDtypeStruct(floe_area.shape, F3...  86.3 us
    unnamed x1, local copies, waits for them, and re-layouts  2.52 us

profile of v3, /device:TPU:1, one launch (start us, length us, event | category | flops | bytes accessed | tf_op | source)
XLA Modules:
  0.0 88.9 jit_solution(16748580075619624707)
XLA Ops:
  0.0 86.3 %shard_map.118 = f32[5,16,8,512]{3,2,1,0:T(8,128)} custom-call(f32[36]{0:T(128)} %decay.1, f32[5,16,8,512]{3,2,1,0:T(8,128)} %floe_hbm.1, f32[2,8,512]{2,1,0:T(8,128)} %courant_hbm.1, bf16[1296,512]{1,0:T(8,128)(2,1)} %bitcast.6, s32[4,4,64]{2,1,0:T(4,128)} %bitcast.7, s32[4,8,512]{2,1,0:T(8,128)} %slot_hbm.1, f32[4,8,512]{2,1,0:T(8,128)} %weight_hbm.1, ...), custom_call_target="tpu_custom_call" | custom-call | tf_op jit(solution)/shard_map/pallas_call | solution.py:422
  86.4 2.5 %copy.14 = f32[5,16,8,512]{3,2,1,0:T(8,128)} copy(f32[5,16,8,512]{3,2,1,0:T(8,128)} %shard_map.118) | data formatting | bytes 2621440

commit v4 on v3

--- a/solution.py
+++ b/solution.py
@@ -15,9 +15,8 @@
 NBIN = 1296
 NSUB = 3
 N_DEV = 256
-SPLIT = 1024
-TAIL = 256
-WIDE = SPLIT + TAIL
+RANGES = ((0, 768), (768, 384), (1152, 128))
+WIDE = 1280
 COLUMN_ROWS = 768
 
 
@@ -36,18 +35,18 @@
     return (lax.rem(x + i // 4, 4) * 16 + zc, lax.rem(s + i % 4, 4))
 
 
-def tile_of(x, zc, dx, dz, dc):
-    core = lax.rem(lax.rem(zc, 2) + dc, 2)
-    return lax.rem(x + dx, 4) * 16 + lax.rem(zc // 2 + dz, 8) * 2 + core
-
-
-def send_all(src, dst, send_sem, recv_sem):
+def zc_numbers(zc):
+    return [
+        lax.rem(zc // 2 + i // 2, 8) * 2 + lax.rem(lax.rem(zc, 2) + i % 2, 2) for i in range(16)
+    ]
+
+
+def sender(src, dst, send_sem, recv_sem):
     x, zc, s = coords()
     me = (zc * 4 + x) * 4 + s
-
-    def one(i, carry):
-        tile = tile_of(x, zc, i // 64, lax.rem(i // 2, 8), lax.rem(i, 2))
-        sub = lax.rem(s + lax.rem(i // 16, 4), 4)
+    numbers = zc_numbers(zc)
+
+    def send(tile, sub):
         pltpu.make_async_remote_copy(
             src_ref=src.at[tile * 4 + sub],
             dst_ref=dst.at[me],
@@ -56,9 +55,28 @@
             device_id=(tile, sub),
             device_id_type=MESH,
         ).start()
-        return carry
-
-    lax.fori_loop(1, N_DEV, one, 0)
+
+    def near():
+        for number in numbers[1:]:
+            send(x * 16 + number, s)
+
+        def one(i, carry):
+            send(lax.rem(x + i // 4, 4) * 16 + zc, lax.rem(s + lax.rem(i, 4), 4))
+            return carry
+
+        lax.fori_loop(1, 16, one, 0)
+
+    def far():
+        def one(i, carry):
+            first = lax.rem(x + i // 4, 4) * 16
+            sub = lax.rem(s + lax.rem(i, 4), 4)
+            for number in numbers[1:]:
+                send(first + number, sub)
+            return carry
+
+        lax.fori_loop(1, 16, one, 0)
+
+    return near, far
 
 
 def send_group(peer, number, src, dst, me, send_sem, recv_sem):
@@ -86,19 +104,22 @@
     choose[...] = jnp.where(cell == column.astype(jnp.int32), 1.0, 0.0).astype(BF16)
 
 
-def gather_rows(choose, spectra, xa, xb, tail_send):
-    over_cells = (((1,), (1,)), ((), ()))
-    for start in range(0, WIDE, 256):
+OVER_CELLS = (((1,), (1,)), ((), ()))
+
+
+def gather_rows(choose, spectra, first, size, dst):
+    for lane in range(0, size, 256):
+        width = min(256, size - lane)
+        start = first + lane
         rows = lax.dot_general(
-            choose[...], spectra[start : start + 256, :], over_cells, preferred_element_type=F32
+            choose[...], spectra[start : start + width, :], OVER_CELLS, preferred_element_type=F32
         )
-        rows = rows.astype(BF16).reshape(N_DEV, 4, 256)
-        if start < SPLIT:
-            xa[:, :, start : start + 256] = rows
-        else:
-            xb[...] = rows
+        dst[:, :, lane : lane + width] = rows.astype(BF16).reshape(N_DEV, 4, width)
+
+
+def gather_tail(choose, spectra, tail_send):
     last = lax.dot_general(
-        choose[...], spectra[WIDE:, :], over_cells, preferred_element_type=F32
+        choose[...], spectra[WIDE:, :], OVER_CELLS, preferred_element_type=F32
     )
     filler = jnp.zeros((64, NBIN - WIDE), F32)
     for zc in range(16):
@@ -291,15 +312,18 @@
             above = above + breakable
 
 
-STEPS_A = [(i * 144, 144) for i in range(6)] + [(864, 160)]
-STEPS_B = [(1024, 128), (1152, 144)]
+STEPS = (
+    ((0, 256), (256, 256), (512, 256)),
+    ((768, 192), (960, 192)),
+    ((1152, 144),),
+)
 
 
 def kernel(
     decay, floe_hbm, courant_hbm, spectra_hbm, picks_hbm, slot_hbm, weight_hbm, thick_hbm, edge_hbm,
     strain_hbm, ice_hbm, brk_hbm, out,
     floe, courant, spectra, picks, slot, weight, thick, edge, strain, ice, brk,
-    choose, xa, xb, ra, rb, tail_send, tail_mid, tail_pass, tail_recv,
+    choose, x0, x1, x2, r0, r1, r2, tail_send, tail_mid, tail_pass, tail_recv,
     row_send, row_recv, col_send, col_recv, side,
     table, mixing, decay_table, paths, att, hist,
     load_sem, send_sem, recv_sem, own_sem, halo_send, halo_recv, group_sem
@@ -327,7 +351,15 @@
     for i in range(1, 16):
         pl.semaphore_signal(group_sem, inc=1, device_id=xy_peer(i, x, zc, s), device_id_type=MESH)
     loads[1].wait()
-    gather_rows(choose, spectra, xa, xb, tail_send)
+    sends, lands = (x0, x1, x2), (r0, r1, r2)
+    senders = [
+        sender(sends[k], lands[k], send_sem.at[k], recv_sem.at[k]) for k in range(3)
+    ]
+    gather_rows(choose, spectra, *RANGES[0], x0)
+    senders[0][0]()
+    gather_rows(choose, spectra, *RANGES[1], x1)
+    gather_rows(choose, spectra, *RANGES[2], x2)
+    gather_tail(choose, spectra, tail_send)
     for copy in loads[2:]:
         copy.wait()
     pack_halo(floe, courant, row_send, col_send)
@@ -343,25 +375,26 @@
     for copy in halo:
         copy.start()
     own = [
-        pltpu.make_async_copy(xa.at[me], ra.at[me_slot], own_sem.at[0]),
-        pltpu.make_async_copy(xb.at[me], rb.at[me_slot], own_sem.at[1]),
-        pltpu.make_async_copy(tail_send.at[zc], tail_mid.at[zc], own_sem.at[2]),
+        pltpu.make_async_copy(sends[k].at[me], lands[k].at[me_slot], own_sem.at[k])
+        for k in range(3)
     ]
+    own.append(pltpu.make_async_copy(tail_send.at[zc], tail_mid.at[zc], own_sem.at[3]))
     for copy in own:
         copy.start()
-    send_group(zc_peer, zc_number, tail_send, tail_mid, zc, send_sem.at[2], recv_sem.at[2])
-    send_all(xa, ra, send_sem.at[0], recv_sem.at[0])
-    send_all(xb, rb, send_sem.at[1], recv_sem.at[1])
+    send_group(zc_peer, zc_number, tail_send, tail_mid, zc, send_sem.at[3], recv_sem.at[3])
+    senders[0][1]()
+    senders[1][0]()
+    senders[1][1]()
 
     fifteen = pl.ds(0, 15)
-    own[2].wait()
-    pltpu.make_async_copy(tail_send.at[fifteen], tail_mid.at[fifteen], recv_sem.at[2]).wait()
+    own[3].wait()
+    pltpu.make_async_copy(tail_send.at[fifteen], tail_mid.at[fifteen], recv_sem.at[3]).wait()
     regroup_tail(tail_mid, tail_pass)
     own_tail = pltpu.make_async_copy(
-        tail_pass.at[x * 4 + s], tail_recv.at[x * 4 + s], own_sem.at[3]
+        tail_pass.at[x * 4 + s], tail_recv.at[x * 4 + s], own_sem.at[4]
     )
     own_tail.start()
-    send_group(xy_peer, xy_number, tail_pass, tail_recv, x * 4 + s, send_sem.at[3], recv_sem.at[3])
+    send_group(xy_peer, xy_number, tail_pass, tail_recv, x * 4 + s, send_sem.at[4], recv_sem.at[4])
 
     fill_decay(decay, decay_table)
     fill_paths(thick, edge, paths)
@@ -376,38 +409,32 @@
     unpack_columns(col_recv, side)
     transport(floe, courant, row_recv, side, out)
 
+    senders[2][0]()
+    senders[2][1]()
     own_tail.wait()
-    pltpu.make_async_copy(tail_pass.at[fifteen], tail_recv.at[fifteen], recv_sem.at[3]).wait()
+    pltpu.make_async_copy(tail_pass.at[fifteen], tail_recv.at[fifteen], recv_sem.at[4]).wait()
     finish_tail(tail_recv, table)
 
     others = pl.ds(0, N_DEV - 1)
-    own[0].wait()
-    pltpu.make_async_copy(xa.at[others], ra.at[others], recv_sem.at[0]).wait()
-    transpose_in(ra, table, 0, SPLIT)
-
-    def row_a(r, carry):
-        attenuate(r, STEPS_A, table, mixing, decay_table, paths, att)
-        part = jnp.dot(strain[:, :SPLIT], att[:SPLIT], preferred_element_type=F32)
-        hist[:, pl.ds(r, 1), :] = part[:, None, :]
-        return carry
-
-    lax.fori_loop(0, 8, row_a, 0)
-    own[1].wait()
-    pltpu.make_async_copy(xb.at[others], rb.at[others], recv_sem.at[1]).wait()
-    transpose_in(rb, table, SPLIT, TAIL)
-
-    def row_b(r, carry):
-        attenuate(r, STEPS_B, table, mixing, decay_table, paths, att)
-        part = jnp.dot(strain[:, SPLIT:], att[SPLIT:], preferred_element_type=F32)
-        hist[:, pl.ds(r, 1), :] += part[:, None, :]
-        return carry
-
-    lax.fori_loop(0, 8, row_b, 0)
+    for k, (first, size) in enumerate(RANGES):
+        own[k].wait()
+        pltpu.make_async_copy(sends[k].at[others], lands[k].at[others], recv_sem.at[k]).wait()
+        transpose_in(lands[k], table, first, size)
+        bins = slice(STEPS[k][0][0], sum(STEPS[k][-1]))
+
+        def one_row(r, carry):
+            attenuate(r, STEPS[k], table, mixing, decay_table, paths, att)
+            part = jnp.dot(strain[:, bins], att[bins], preferred_element_type=F32)[:, None, :]
+            here = pl.ds(r, 1)
+            hist[:, here, :] = part if k == 0 else hist[:, here, :] + part
+            return carry
+
+        lax.fori_loop(0, 8, one_row, 0)
     fracture(hist, weight, ice, brk, out)
-    pltpu.make_async_copy(xa.at[others], ra.at[others], send_sem.at[0]).wait()
-    pltpu.make_async_copy(xb.at[others], rb.at[others], send_sem.at[1]).wait()
-    pltpu.make_async_copy(tail_send.at[fifteen], tail_mid.at[fifteen], send_sem.at[2]).wait()
-    pltpu.make_async_copy(tail_pass.at[fifteen], tail_recv.at[fifteen], send_sem.at[3]).wait()
+    for k in range(3):
+        pltpu.make_async_copy(sends[k].at[others], lands[k].at[others], send_sem.at[k]).wait()
+    pltpu.make_async_copy(tail_send.at[fifteen], tail_mid.at[fifteen], send_sem.at[3]).wait()
+    pltpu.make_async_copy(tail_pass.at[fifteen], tail_recv.at[fifteen], send_sem.at[4]).wait()
 
 
 def shards(
@@ -428,10 +455,8 @@
         scratch_shapes=[pltpu.VMEM(v.shape, v.dtype) for v in operands]
         + [
             pltpu.VMEM((N_DEV * 4, 512), BF16),
-            pltpu.VMEM((N_DEV, 4, SPLIT), BF16),
-            pltpu.VMEM((N_DEV, 4, TAIL), BF16),
-            pltpu.VMEM((N_DEV, 4, SPLIT), BF16),
-            pltpu.VMEM((N_DEV, 4, TAIL), BF16),
+            *[pltpu.VMEM((N_DEV, 4, size), BF16) for _, size in RANGES],
+            *[pltpu.VMEM((N_DEV, 4, size), BF16) for _, size in RANGES],
             pltpu.VMEM((16, 16, 128), BF16),
             pltpu.VMEM((16, 16, 128), BF16),
             pltpu.VMEM((16, 4, 256), BF16),
@@ -448,9 +473,9 @@
             pltpu.VMEM((NBIN, 512), BF16),
             pltpu.VMEM((16, 8, 512), F32),
             pltpu.SemaphoreType.DMA((len(operands),)),
-            pltpu.SemaphoreType.DMA((4,)),
-            pltpu.SemaphoreType.DMA((4,)),
-            pltpu.SemaphoreType.DMA((4,)),
+            pltpu.SemaphoreType.DMA((5,)),
+            pltpu.SemaphoreType.DMA((5,)),
+            pltpu.SemaphoreType.DMA((5,)),
             pltpu.SemaphoreType.DMA((8,)),
             pltpu.SemaphoreType.DMA((8,)),
             pltpu.SemaphoreType.REGULAR,

time: 89 us -> 84.7 us (0.952)
  Pallas kernels: 86.3 us -> 82 us
    pallas_call x1, Pallas kernels: 86.3 us -> 82 us  [shards(): pl.pallas_call(kernel, out_shape=jax.ShapeDtypeStruct(floe_area.shape, F3...]
where the time goes in v4:
time: 84.7 us; the launch traced here: 84.6 us
  Pallas kernels  82 us (97%)
  local copies, waits for them, and re-layouts  2.52 us (3%)
    pallas_call x1, Pallas kernels, shards(): pl.pallas_call(kernel, out_shape=jax.ShapeDtypeStruct(floe_area.shape, F3...  82 us
    unnamed x1, local copies, waits for them, and re-layouts  2.52 us

profile of v4, /device:TPU:1, one launch (start us, length us, event | category | flops | bytes accessed | tf_op | source)
XLA Modules:
  0.0 84.6 jit_solution(1247257724859140901)
XLA Ops:
  0.0 82.0 %shard_map.118 = f32[5,16,8,512]{3,2,1,0:T(8,128)} custom-call(f32[36]{0:T(128)} %decay.1, f32[5,16,8,512]{3,2,1,0:T(8,128)} %floe_hbm.1, f32[2,8,512]{2,1,0:T(8,128)} %courant_hbm.1, bf16[1296,512]{1,0:T(8,128)(2,1)} %bitcast.6, s32[4,4,64]{2,1,0:T(4,128)} %bitcast.7, s32[4,8,512]{2,1,0:T(8,128)} %slot_hbm.1, f32[4,8,512]{2,1,0:T(8,128)} %weight_hbm.1, ...), custom_call_target="tpu_custom_call" | custom-call | tf_op jit(solution)/shard_map/pallas_call | solution.py:449
  82.1 2.5 %copy.14 = f32[5,16,8,512]{3,2,1,0:T(8,128)} copy(f32[5,16,8,512]{3,2,1,0:T(8,128)} %shard_map.118) | data formatting | bytes 2621440

commit v5 on v4

--- a/solution.py
+++ b/solution.py
@@ -289,7 +289,7 @@
         att[start : start + size, :] = (spectrum * jnp.exp2(decay_rows * factor)).astype(BF16)
 
 
-def fracture(hist, weight, ice, brk, out):
+def fracture(hist, weight, ice, brk, out, out_hbm, out_sem):
     total_w = weight[0] + weight[1] + weight[2] + weight[3]
     used_w = sum(weight[k].astype(BF16).astype(F32) for k in range(4))
     fix = total_w / used_w
@@ -310,6 +310,7 @@
             breakable = jnp.where(brk_rows <= k, value, 0.0)
             out[n, k] = value - breakable * shorter[k] + above * share[k]
             above = above + breakable
+        pltpu.make_async_copy(out.at[n], out_hbm.at[n], out_sem.at[n]).start()
 
 
 STEPS = (
@@ -317,16 +318,17 @@
     ((768, 192), (960, 192)),
     ((1152, 144),),
 )
+UNROLL = (2, 2, 4)
 
 
 def kernel(
-    decay, floe_hbm, courant_hbm, spectra_hbm, picks_hbm, slot_hbm, weight_hbm, thick_hbm, edge_hbm,
-    strain_hbm, ice_hbm, brk_hbm, out,
-    floe, courant, spectra, picks, slot, weight, thick, edge, strain, ice, brk,
+    decay_hbm, floe_hbm, courant_hbm, spectra_hbm, picks_hbm, slot_hbm, weight_hbm, thick_hbm, edge_hbm,
+    strain_hbm, ice_hbm, brk_hbm, out_hbm,
+    decay, floe, courant, spectra, picks, slot, weight, thick, edge, strain, ice, brk, out,
     choose, x0, x1, x2, r0, r1, r2, tail_send, tail_mid, tail_pass, tail_recv,
     row_send, row_recv, col_send, col_recv, side,
     table, mixing, decay_table, paths, att, hist,
-    load_sem, send_sem, recv_sem, own_sem, halo_send, halo_recv, group_sem
+    load_sem, send_sem, recv_sem, own_sem, halo_send, halo_recv, out_sem, group_sem
 ):
     x, zc, s = coords()
     me = (x * 16 + zc) * 4 + s
@@ -338,7 +340,7 @@
     pairs = (
         (picks_hbm, picks), (spectra_hbm, spectra), (floe_hbm, floe), (courant_hbm, courant),
         (slot_hbm, slot), (weight_hbm, weight), (thick_hbm, thick), (edge_hbm, edge),
-        (strain_hbm, strain), (ice_hbm, ice), (brk_hbm, brk),
+        (strain_hbm, strain), (ice_hbm, ice), (brk_hbm, brk), (decay_hbm, decay),
     )
     loads = [
         pltpu.make_async_copy(src, dst, load_sem.at[k]) for k, (src, dst) in enumerate(pairs)
@@ -357,8 +359,6 @@
     ]
     gather_rows(choose, spectra, *RANGES[0], x0)
     senders[0][0]()
-    gather_rows(choose, spectra, *RANGES[1], x1)
-    gather_rows(choose, spectra, *RANGES[2], x2)
     gather_tail(choose, spectra, tail_send)
     for copy in loads[2:]:
         copy.wait()
@@ -379,12 +379,10 @@
         for k in range(3)
     ]
     own.append(pltpu.make_async_copy(tail_send.at[zc], tail_mid.at[zc], own_sem.at[3]))
-    for copy in own:
-        copy.start()
+    own[3].start()
     send_group(zc_peer, zc_number, tail_send, tail_mid, zc, send_sem.at[3], recv_sem.at[3])
     senders[0][1]()
-    senders[1][0]()
-    senders[1][1]()
+    own[0].start()
 
     fifteen = pl.ds(0, 15)
     own[3].wait()
@@ -395,6 +393,11 @@
     )
     own_tail.start()
     send_group(xy_peer, xy_number, tail_pass, tail_recv, x * 4 + s, send_sem.at[4], recv_sem.at[4])
+    for k in (1, 2):
+        gather_rows(choose, spectra, *RANGES[k], sends[k])
+        own[k].start()
+    senders[1][0]()
+    senders[1][1]()
 
     fill_decay(decay, decay_table)
     fill_paths(thick, edge, paths)
@@ -411,30 +414,36 @@
 
     senders[2][0]()
     senders[2][1]()
-    own_tail.wait()
-    pltpu.make_async_copy(tail_pass.at[fifteen], tail_recv.at[fifteen], recv_sem.at[4]).wait()
-    finish_tail(tail_recv, table)
-
     others = pl.ds(0, N_DEV - 1)
     for k, (first, size) in enumerate(RANGES):
+        if k == 2:
+            own_tail.wait()
+            pltpu.make_async_copy(
+                tail_pass.at[fifteen], tail_recv.at[fifteen], recv_sem.at[4]
+            ).wait()
+            finish_tail(tail_recv, table)
         own[k].wait()
         pltpu.make_async_copy(sends[k].at[others], lands[k].at[others], recv_sem.at[k]).wait()
         transpose_in(lands[k], table, first, size)
         bins = slice(STEPS[k][0][0], sum(STEPS[k][-1]))
 
-        def one_row(r, carry):
-            attenuate(r, STEPS[k], table, mixing, decay_table, paths, att)
-            part = jnp.dot(strain[:, bins], att[bins], preferred_element_type=F32)[:, None, :]
-            here = pl.ds(r, 1)
-            hist[:, here, :] = part if k == 0 else hist[:, here, :] + part
+        def some_rows(i, carry):
+            for u in range(UNROLL[k]):
+                r = i * UNROLL[k] + u
+                attenuate(r, STEPS[k], table, mixing, decay_table, paths, att.at[u])
+                part = jnp.dot(strain[:, bins], att[u, bins], preferred_element_type=F32)
+                here = pl.ds(r, 1)
+                hist[:, here, :] = part[:, None] if k == 0 else hist[:, here, :] + part[:, None]
             return carry
 
-        lax.fori_loop(0, 8, one_row, 0)
-    fracture(hist, weight, ice, brk, out)
+        lax.fori_loop(0, 8 // UNROLL[k], some_rows, 0)
+    fracture(hist, weight, ice, brk, out, out_hbm, out_sem)
     for k in range(3):
         pltpu.make_async_copy(sends[k].at[others], lands[k].at[others], send_sem.at[k]).wait()
     pltpu.make_async_copy(tail_send.at[fifteen], tail_mid.at[fifteen], send_sem.at[3]).wait()
     pltpu.make_async_copy(tail_pass.at[fifteen], tail_recv.at[fifteen], send_sem.at[4]).wait()
+    for n in range(5):
+        pltpu.make_async_copy(out.at[n], out_hbm.at[n], out_sem.at[n]).wait()
 
 
 def shards(
@@ -445,14 +454,14 @@
         floe_area, courant, spectra[0, 0].T, jnp.transpose(send_rows[0, 0], (1, 2, 0)), src_slot,
         src_weight, thickness, edge_angle, strain_table, ice_mask, break_bin
     )
-    vmem = pl.BlockSpec(memory_space=pltpu.VMEM)
+    anywhere = pl.BlockSpec(memory_space=pl.ANY)
     return pl.pallas_call(
         kernel,
         out_shape=jax.ShapeDtypeStruct(floe_area.shape, F32),
-        in_specs=[pl.BlockSpec(memory_space=pltpu.SMEM)]
-        + [pl.BlockSpec(memory_space=pl.ANY)] * len(operands),
-        out_specs=vmem,
-        scratch_shapes=[pltpu.VMEM(v.shape, v.dtype) for v in operands]
+        in_specs=[anywhere] * (len(operands) + 1),
+        out_specs=anywhere,
+        scratch_shapes=[pltpu.SMEM(decay_rate.shape, F32)]
+        + [pltpu.VMEM(v.shape, v.dtype) for v in (*operands, floe_area)]
         + [
             pltpu.VMEM((N_DEV * 4, 512), BF16),
             *[pltpu.VMEM((N_DEV, 4, size), BF16) for _, size in RANGES],
@@ -470,14 +479,15 @@
             pltpu.VMEM((8, N_DEV * 4, 512), BF16),
             pltpu.VMEM((NBIN, 128), F32),
             pltpu.VMEM((8, 72, 512), F32),
-            pltpu.VMEM((NBIN, 512), BF16),
+            pltpu.VMEM((4, NBIN, 512), BF16),
             pltpu.VMEM((16, 8, 512), F32),
-            pltpu.SemaphoreType.DMA((len(operands),)),
+            pltpu.SemaphoreType.DMA((len(operands) + 1,)),
             pltpu.SemaphoreType.DMA((5,)),
             pltpu.SemaphoreType.DMA((5,)),
             pltpu.SemaphoreType.DMA((5,)),
             pltpu.SemaphoreType.DMA((8,)),
             pltpu.SemaphoreType.DMA((8,)),
+            pltpu.SemaphoreType.DMA((5,)),
             pltpu.SemaphoreType.REGULAR,
         ],
         compiler_params=pltpu.CompilerParams(

time: 84.7 us -> 82.4 us (0.973)
  Pallas kernels: 82 us -> 79.7 us
    pallas_call x1, Pallas kernels: 82 us -> 79.7 us  [shards(): pl.pallas_call(kernel, out_shape=jax.ShapeDtypeStruct(floe_area.shape, F3...]
where the time goes in v5:
time: 82.4 us; the launch traced here: 82.3 us
  Pallas kernels  79.7 us (97%)
  local copies, waits for them, and re-layouts  2.52 us (3%)
    pallas_call x1, Pallas kernels, shards(): pl.pallas_call(kernel, out_shape=jax.ShapeDtypeStruct(floe_area.shape, F3...  79.7 us
    unnamed x1, local copies, waits for them, and re-layouts  2.52 us

profile of v5, /device:TPU:1, one launch (start us, length us, event | category | flops | bytes accessed | tf_op | source)
XLA Modules:
  0.0 82.3 jit_solution(17068017516923131701)
XLA Ops:
  0.0 79.7 %shard_map.118 = f32[5,16,8,512]{3,2,1,0:T(8,128)} custom-call(f32[36]{0:T(128)} %decay_hbm.1, f32[5,16,8,512]{3,2,1,0:T(8,128)} %floe_hbm.1, f32[2,8,512]{2,1,0:T(8,128)} %courant_hbm.1, bf16[1296,512]{1,0:T(8,128)(2,1)} %bitcast.6, s32[4,4,64]{2,1,0:T(4,128)} %bitcast.7, s32[4,8,512]{2,1,0:T(8,128)} %slot_hbm.1, f32[4,8,512]{2,1,0:T(8,128)} %weight_hbm.1, ...), custom_call_target="tpu_custom_call" | custom-call | tf_op jit(solution)/shard_map/pallas_call | solution.py:458
  79.8 2.5 %copy.14 = f32[5,16,8,512]{3,2,1,0:T(8,128)} copy(f32[5,16,8,512]{3,2,1,0:T(8,128)} %shard_map.118) | data formatting | bytes 2621440

commit v6 on v5

--- a/solution.py
+++ b/solution.py
@@ -275,21 +275,24 @@
         paths[r] = scaled[r : r + 1] / (0.25 + 0.75 * cosine * cosine)
 
 
-def attenuate(r, steps, table, mixing, decay_table, paths, att):
+def damping(r, start, size, decay_table, paths):
     path = paths[r]
+    first = start % 72
+    pieces, have = [path[first:]], 72 - first
+    while have < size:
+        pieces.append(path)
+        have += 72
+    factor = jnp.concatenate(pieces, axis=0)[:size]
+    return jnp.exp2(wide(decay_table[start : start + size, :]) * factor)
+
+
+def attenuate(r, steps, table, mixing, damp, att):
     for start, size in steps:
         spectrum = jnp.dot(table[start : start + size, :], mixing[r], preferred_element_type=F32)
-        decay_rows = wide(decay_table[start : start + size, :])
-        first = start % 72
-        pieces, have = [path[first:]], 72 - first
-        while have < size:
-            pieces.append(path)
-            have += 72
-        factor = jnp.concatenate(pieces, axis=0)[:size]
-        att[start : start + size, :] = (spectrum * jnp.exp2(decay_rows * factor)).astype(BF16)
-
-
-def fracture(hist, weight, ice, brk, out, out_hbm, out_sem):
+        att[start : start + size, :] = (spectrum * damp(r, start, size)).astype(BF16)
+
+
+def fracture(hist, weight, ice, brk, out):
     total_w = weight[0] + weight[1] + weight[2] + weight[3]
     used_w = sum(weight[k].astype(BF16).astype(F32) for k in range(4))
     fix = total_w / used_w
@@ -310,7 +313,6 @@
             breakable = jnp.where(brk_rows <= k, value, 0.0)
             out[n, k] = value - breakable * shorter[k] + above * share[k]
             above = above + breakable
-        pltpu.make_async_copy(out.at[n], out_hbm.at[n], out_sem.at[n]).start()
 
 
 STEPS = (
@@ -323,12 +325,12 @@
 
 def kernel(
     decay_hbm, floe_hbm, courant_hbm, spectra_hbm, picks_hbm, slot_hbm, weight_hbm, thick_hbm, edge_hbm,
-    strain_hbm, ice_hbm, brk_hbm, out_hbm,
-    decay, floe, courant, spectra, picks, slot, weight, thick, edge, strain, ice, brk, out,
+    strain_hbm, ice_hbm, brk_hbm, out,
+    decay, floe, courant, spectra, picks, slot, weight, thick, edge, strain, ice, brk,
     choose, x0, x1, x2, r0, r1, r2, tail_send, tail_mid, tail_pass, tail_recv,
     row_send, row_recv, col_send, col_recv, side,
-    table, mixing, decay_table, paths, att, hist,
-    load_sem, send_sem, recv_sem, own_sem, halo_send, halo_recv, out_sem, group_sem
+    table, mixing, decay_table, paths, last_damping, att, hist,
+    load_sem, send_sem, recv_sem, own_sem, halo_send, halo_recv, group_sem
 ):
     x, zc, s = coords()
     me = (x * 16 + zc) * 4 + s
@@ -404,6 +406,7 @@
 
     def mix_row(r, carry):
         build_mixing(r, slot, weight, mixing)
+        last_damping[r] = damping(r, *STEPS[2][0], decay_table, paths)
         return carry
 
     lax.fori_loop(0, 8, mix_row, 0)
@@ -414,6 +417,11 @@
 
     senders[2][0]()
     senders[2][1]()
+    def damp(r, start, size):
+        if (start, size) == STEPS[2][0]:
+            return last_damping[r]
+        return damping(r, start, size, decay_table, paths)
+
     others = pl.ds(0, N_DEV - 1)
     for k, (first, size) in enumerate(RANGES):
         if k == 2:
@@ -430,20 +438,18 @@
         def some_rows(i, carry):
             for u in range(UNROLL[k]):
                 r = i * UNROLL[k] + u
-                attenuate(r, STEPS[k], table, mixing, decay_table, paths, att.at[u])
+                attenuate(r, STEPS[k], table, mixing, damp, att.at[u])
                 part = jnp.dot(strain[:, bins], att[u, bins], preferred_element_type=F32)
                 here = pl.ds(r, 1)
                 hist[:, here, :] = part[:, None] if k == 0 else hist[:, here, :] + part[:, None]
             return carry
 
         lax.fori_loop(0, 8 // UNROLL[k], some_rows, 0)
-    fracture(hist, weight, ice, brk, out, out_hbm, out_sem)
+    fracture(hist, weight, ice, brk, out)
     for k in range(3):
         pltpu.make_async_copy(sends[k].at[others], lands[k].at[others], send_sem.at[k]).wait()
     pltpu.make_async_copy(tail_send.at[fifteen], tail_mid.at[fifteen], send_sem.at[3]).wait()
     pltpu.make_async_copy(tail_pass.at[fifteen], tail_recv.at[fifteen], send_sem.at[4]).wait()
-    for n in range(5):
-        pltpu.make_async_copy(out.at[n], out_hbm.at[n], out_sem.at[n]).wait()
 
 
 def shards(
@@ -457,11 +463,11 @@
     anywhere = pl.BlockSpec(memory_space=pl.ANY)
     return pl.pallas_call(
         kernel,
-        out_shape=jax.ShapeDtypeStruct(floe_area.shape, F32),
+        out_shape=pltpu.VMEM(floe_area.shape, F32),
         in_specs=[anywhere] * (len(operands) + 1),
-        out_specs=anywhere,
+        out_specs=pl.BlockSpec(memory_space=pltpu.VMEM),
         scratch_shapes=[pltpu.SMEM(decay_rate.shape, F32)]
-        + [pltpu.VMEM(v.shape, v.dtype) for v in (*operands, floe_area)]
+        + [pltpu.VMEM(v.shape, v.dtype) for v in operands]
         + [
             pltpu.VMEM((N_DEV * 4, 512), BF16),
             *[pltpu.VMEM((N_DEV, 4, size), BF16) for _, size in RANGES],
@@ -479,6 +485,7 @@
             pltpu.VMEM((8, N_DEV * 4, 512), BF16),
             pltpu.VMEM((NBIN, 128), F32),
             pltpu.VMEM((8, 72, 512), F32),
+            pltpu.VMEM((8, STEPS[2][0][1], 512), F32),
             pltpu.VMEM((4, NBIN, 512), BF16),
             pltpu.VMEM((16, 8, 512), F32),
             pltpu.SemaphoreType.DMA((len(operands) + 1,)),
@@ -487,7 +494,6 @@
             pltpu.SemaphoreType.DMA((5,)),
             pltpu.SemaphoreType.DMA((8,)),
             pltpu.SemaphoreType.DMA((8,)),
-            pltpu.SemaphoreType.DMA((5,)),
             pltpu.SemaphoreType.REGULAR,
         ],
         compiler_params=pltpu.CompilerParams(

time: 82.4 us -> 80 us (0.971)
  local copies, waits for them, and re-layouts: 2.52 us -> 1.06 us
  Pallas kernels: 79.7 us -> 78.8 us
    unnamed x1, local copies, waits for them, and re-layouts: 2.52 us -> 1.06 us
    pallas_call x1, Pallas kernels: 79.7 us -> 78.8 us  [shards(): pl.pallas_call(kernel, out_shape=pltpu.VMEM(floe_area.shape, F32), in_spe...]
where the time goes in v6:
time: 80 us; the launch traced here: 79.9 us
  Pallas kernels  78.8 us (98%)
  local copies, waits for them, and re-layouts  1.06 us (1%)
    pallas_call x1, Pallas kernels, shards(): pl.pallas_call(kernel, out_shape=pltpu.VMEM(floe_area.shape, F32), in_spe...  78.8 us

profile of v6, /device:TPU:1, one launch (start us, length us, event | category | flops | bytes accessed | tf_op | source)
XLA Modules:
  0.0 79.9 jit_solution(1061720793622677068)
XLA Ops:
  0.0 78.8 %shard_map.118 = f32[5,16,8,512]{3,2,1,0:T(8,128)S(1)} custom-call(f32[36]{0:T(128)} %decay_hbm.1, f32[5,16,8,512]{3,2,1,0:T(8,128)} %floe_hbm.1, f32[2,8,512]{2,1,0:T(8,128)} %courant_hbm.1, bf16[1296,512]{1,0:T(8,128)(2,1)} %bitcast.6, s32[4,4,64]{2,1,0:T(4,128)} %bitcast.7, s32[4,8,512]{2,1,0:T(8,128)} %slot_hbm.1, f32[4,8,512]{2,1,0:T(8,128)} %weight_hbm.1, ...), custom_call_target="tpu_custom_call" | custom-call | tf_op jit(solution)/shard_map/pallas_call | solution.py:464
  78.9 1.1 %copy.14 = f32[5,16,8,512]{3,2,1,0:T(8,128)} copy(f32[5,16,8,512]{3,2,1,0:T(8,128)S(1)} %shard_map.118) | data formatting | bytes 2621440

commit v7 on v6

--- a/solution.py
+++ b/solution.py
@@ -15,7 +15,7 @@
 NBIN = 1296
 NSUB = 3
 N_DEV = 256
-RANGES = ((0, 768), (768, 384), (1152, 128))
+RANGES = ((0, 896), (896, 256), (1152, 128))
 WIDE = 1280
 COLUMN_ROWS = 768
 
@@ -316,11 +316,11 @@
 
 
 STEPS = (
-    ((0, 256), (256, 256), (512, 256)),
-    ((768, 192), (960, 192)),
+    ((0, 256), (256, 320), (576, 320)),
+    ((896, 256),),
     ((1152, 144),),
 )
-UNROLL = (2, 2, 4)
+UNROLL = (2, 2, 8)
 
 
 def kernel(
@@ -486,7 +486,7 @@
             pltpu.VMEM((NBIN, 128), F32),
             pltpu.VMEM((8, 72, 512), F32),
             pltpu.VMEM((8, STEPS[2][0][1], 512), F32),
-            pltpu.VMEM((4, NBIN, 512), BF16),
+            pltpu.VMEM((8, NBIN, 512), BF16),
             pltpu.VMEM((16, 8, 512), F32),
             pltpu.SemaphoreType.DMA((len(operands) + 1,)),
             pltpu.SemaphoreType.DMA((5,)),

time: 80 us -> 80 us (level)
  no operation moved by 1% of the time
where the time goes in v7:
time: 80 us; the launch traced here: 79.9 us
  Pallas kernels  78.8 us (98%)
  local copies, waits for them, and re-layouts  1.06 us (1%)
    pallas_call x1, Pallas kernels, shards(): pl.pallas_call(kernel, out_shape=pltpu.VMEM(floe_area.shape, F32), in_spe...  78.8 us

profile of v7, /device:TPU:1, one launch (start us, length us, event | category | flops | bytes accessed | tf_op | source)
XLA Modules:
  0.0 79.9 jit_solution(3591325960216669158)
XLA Ops:
  0.0 78.8 %shard_map.118 = f32[5,16,8,512]{3,2,1,0:T(8,128)S(1)} custom-call(f32[36]{0:T(128)} %decay_hbm.1, f32[5,16,8,512]{3,2,1,0:T(8,128)} %floe_hbm.1, f32[2,8,512]{2,1,0:T(8,128)} %courant_hbm.1, bf16[1296,512]{1,0:T(8,128)(2,1)} %bitcast.6, s32[4,4,64]{2,1,0:T(4,128)} %bitcast.7, s32[4,8,512]{2,1,0:T(8,128)} %slot_hbm.1, f32[4,8,512]{2,1,0:T(8,128)} %weight_hbm.1, ...), custom_call_target="tpu_custom_call" | custom-call | tf_op jit(solution)/shard_map/pallas_call | solution.py:464
  78.8 1.1 %copy.14 = f32[5,16,8,512]{3,2,1,0:T(8,128)} copy(f32[5,16,8,512]{3,2,1,0:T(8,128)S(1)} %shard_map.118) | data formatting | bytes 2621440
